TPU v7x, 32 devices: a whole 2x2x4 slice. The times are simulated.
32 devices in a mesh: prow: 4 (over z), pcol: 8 (over y, x, core).
Axes of the slice: x: 2, y: 2, z: 4, core: 2. Of those that a mesh axis runs over, the one named last changes fastest.
Arguments:
- ancestor_inv: float32 [16384, 16384], P('prow', 'pcol'), may hold values from -0.15625 to 0.15625
- l_scaled: float32 [2, 1536, 512], P(None, 'prow'), may hold values from -0.9 to 0.9
- diag_inv: float32 [2, 512, 512], replicated, may hold values from -6 to 6
- tile_lists: int32 [2, 6], replicated, may hold values from 0 to 63, as said below
Outputs:
- offdiag: float32 [2, 1536, 512], P(None, ('prow', 'pcol'))
- diag_block: float32 [2, 512, 512], replicated
Inputs may be any that keep to these rules, and one draw needn't show every extreme that they name: `tile_lists`: each row holds 6 different tile numbers; tile 0 and tile 64 - 1 are in every row.
All inputs are finite; a program needn't handle non-finite values.
Results may differ from a plain program's by a relative error of at most 0.0001.
Values sent between devices are 32-bit elements; how exact they have to be, the bound alone decides.
A program may use at most 192 MiB of HBM per device.

v0:
```python
import jax
import jax.numpy as jnp
from jax import lax
from jax.sharding import PartitionSpec as P

TILE = 256
W = 512
NS = 6
NSUP = 2


def per_device(ancestor_inv, l_scaled, diag_inv, tile_lists):
    highest = lax.Precision.HIGHEST
    tile_rows = ancestor_inv.shape[0] // TILE
    tile_cols = ancestor_inv.shape[1] // TILE
    row_pos = lax.axis_index("prow")
    col_pos = lax.axis_index("pcol")
    grid_tiles = ancestor_inv.reshape(tile_rows, TILE, tile_cols, TILE)
    row_ids = row_pos * tile_rows + jnp.arange(tile_rows, dtype=jnp.int32)
    col_ids = col_pos * tile_cols + jnp.arange(tile_cols, dtype=jnp.int32)
    offs = []
    diags = []
    for index in range(NSUP):
        lfull = lax.all_gather(l_scaled[index], "prow", axis=0, tiled=True)
        total_rows = lfull.shape[0]
        listed = tile_lists[index]
        pick_col = (listed[None, :] == col_ids[:, None]).astype(jnp.float32)
        picked = jnp.dot(
            pick_col,
            lfull.reshape(NS, TILE * W),
            precision=highest,
            preferred_element_type=jnp.float32,
        )
        picked = picked.reshape(tile_cols, TILE, W)
        products = jnp.einsum(
            "aibj,bjw->aiw",
            grid_tiles,
            picked,
            precision=highest,
            preferred_element_type=jnp.float32,
        )
        pick_row = (listed[:, None] == row_ids[None, :]).astype(jnp.float32)
        partial_sum = -jnp.dot(
            pick_row,
            products.reshape(tile_rows, TILE * W),
            precision=highest,
            preferred_element_type=jnp.float32,
        )
        partial_sum = partial_sum.reshape(total_rows, W)
        mine = lax.psum_scatter(partial_sum, ("prow", "pcol"), scatter_dimension=0, tiled=True)
        count = mine.shape[0]
        start = lax.axis_index(("prow", "pcol")) * count
        own_l = lax.dynamic_slice_in_dim(lfull, start, count, 0)
        term = jnp.dot(own_l.T, mine, precision=highest, preferred_element_type=jnp.float32)
        summed = lax.psum(term, ("prow", "pcol"))
        offs.append(mine)
        diags.append(diag_inv[index] - summed)
    return (jnp.stack(offs), jnp.stack(diags))


def solution(mesh):
    placed = (P("prow", "pcol"), P(None, "prow", None), P(), P())
    return jax.shard_map(
        per_device,
        mesh=mesh,
        in_specs=placed,
        out_specs=(P(None, ("prow", "pcol"), None), P()),
        check_vma=False,
    )
```

profile of v0, /device:TPU:0, one launch (start us, length us, event | category | flops | bytes accessed | tf_op | source)
XLA Modules:
  0.0 531.2 jit_solution(12535448123360049787)
XLA Ops:
  7.2 0.0 all-gather.7.cloned.1.call-start
  7.2 2.6 fusion.36
  9.8 0.0 all-gather.7.cloned.1.call-update
  9.9 0.0 all-gather.5.cloned.1.call-start
  9.9 0.7 all-gather.5.cloned.1.call-update
  10.6 0.0 reduce-scatter.5.cloned.1.call-start
  10.7 30.1 %copy.26 = f32[512,8,8,256]{3,2,1,0:T(8,128)} copy(f32[512,8,8,256]{3,1,2,0:T(8,128)} %bitcast.74) | data formatting | bytes 67108864
  40.8 35.1 %copy.15 = f32[16,256,8,256]{1,2,3,0:T(8,128)} copy(f32[16,256,8,256]{3,2,1,0:T(8,128)} %bitcast.73) | data formatting | bytes 67108864 | tf_op jit(solution)/shard_map/reshape | solution.py:18
  75.8 0.0 copy-done.10
  75.8 0.5 slice_bitcast_fusion.1
  76.3 0.5 iota_add_fusion.1
  76.9 5.6 %reshape.43 = f32[6,131072]{1,0:T(8,128)} reshape(f32[1,1536,512]{2,1,0:T(8,128)} %all-gather.7.cloned.1.call-done) | data formatting | bytes 6291456 | tf_op jit(solution)/shard_map/reshape | solution.py:30
  82.5 4.7 fusion.18
  87.2 0.0 copy-done.4
  87.2 0.0 copy-done.6
  87.2 59.7 %fusion.7 = f32[16,256,512]{1,2,0:T(8,128)} fusion(f32[16,256,8,256]{1,2,3,0:T(8,128)} %copy.15, f32[8,256,512]{2,0,1:T(8,128)S(1)} %fusion.18), kind=kOutput, calls=%fused_computation.7 | convolution fusion | flops 51539607552 | bytes 46137344 | tf_op jit(solution)/shard_map/aibj,bjw->aiw/dot_general | solution.py:35
  146.9 0.0 copy-start.5
  146.9 0.0 copy-start.8
  146.9 10.5 %copy.28 = f32[2,8,256,512]{3,1,2,0:T(8,128)} copy(f32[2,8,256,512]{2,3,1,0:T(8,128)} %bitcast.80) | data formatting | bytes 16777216
  157.4 0.0 copy-done.5
  157.4 0.0 copy-done.8
  157.4 8.4 %convolution_negate_fusion = f32[6,131072]{1,0:T(8,128)} fusion(f32[16,131072]{1,0:T(8,128)} %bitcast.76, s32[16]{0:T(128)S(1)} %copy-done.8, s32[6]{0:T(128)S(1)} %copy-done.5), kind=kOutput, calls=%fused_computation | convolution fusion | flops 151781472 | bytes 11534424 | tf_op jit(solution)/shard_map/dot_general | solution.py:43
  165.9 5.4 %reshape.45 = f32[1536,512]{1,0:T(8,128)} reshape(f32[6,131072]{1,0:T(8,128)} %convolution_negate_fusion) | data formatting | bytes 6291456 | tf_op jit(solution)/shard_map/reshape | solution.py:49
  171.3 0.0 reduce-scatter.5.cloned.1.call-update
  171.3 0.0 copy-start.2
  171.3 0.0 reduce-scatter.3.cloned.1.call-start
  171.4 0.0 all-gather.5.cloned.1.call-done
  171.4 5.6 %reshape.39 = f32[6,131072]{1,0:T(8,128)} reshape(f32[1,1536,512]{2,1,0:T(8,128)} %all-gather.5.cloned.1.call-done) | data formatting | bytes 6291456 | tf_op jit(solution)/shard_map/reshape | solution.py:30
  177.0 0.0 copy-done.2
  177.0 4.4 fusion.20
  181.4 59.6 %fusion.4 = f32[16,256,512]{1,2,0:T(8,128)} fusion(f32[16,256,8,256]{1,2,3,0:T(8,128)} %copy.15, f32[8,256,512]{2,0,1:T(8,128)S(1)} %fusion.20), kind=kOutput, calls=%fused_computation.6 | convolution fusion | flops 51539607552 | bytes 46137344 | tf_op jit(solution)/shard_map/aibj,bjw->aiw/dot_general | solution.py:35
  241.1 0.0 copy-start.3
  241.1 10.5 %copy.27 = f32[2,8,256,512]{3,1,2,0:T(8,128)} copy(f32[2,8,256,512]{2,3,1,0:T(8,128)} %bitcast.79) | data formatting | bytes 16777216
  251.7 0.0 copy-done.9
  251.7 8.6 %convolution_negate_fusion.1 = f32[6,131072]{1,0:T(8,128)} fusion(f32[16,131072]{1,0:T(8,128)} %bitcast.75, s32[16]{0:T(128)S(1)} %copy-done.9, s32[6]{0:T(128)S(1)} %copy-done.3), kind=kOutput, calls=%fused_computation.1 | convolution fusion | flops 151781472 | bytes 11534424 | tf_op jit(solution)/shard_map/dot_general | solution.py:43
  260.2 5.4 %reshape.42 = f32[1536,512]{1,0:T(8,128)} reshape(f32[6,131072]{1,0:T(8,128)} %convolution_negate_fusion.1) | data formatting | bytes 6291456 | tf_op jit(solution)/shard_map/reshape | solution.py:49
  265.7 0.0 reduce-scatter.3.cloned.1.call-update
  265.7 0.0 all-reduce.3.cloned.1.call-start
  265.7 10.2 %reduce-scatter.5.cloned.1.call-done = f32[48,512]{1,0:T(8,128)} async-done(((f32[1536,512]{1,0:T(8,128)}), f32[48,512]{1,0:T(8,128)}) %reduce-scatter.5.cloned.1.call-update) | async-done | bytes 98320 | tf_op jit(solution)/shard_map/reduce_scatter | solution.py:50
  275.9 3.0 fusion.12
  278.9 102.8 %reduce-scatter.3.cloned.1.call-done = f32[48,512]{1,0:T(8,128)} async-done(((f32[1536,512]{1,0:T(8,128)}), f32[48,512]{1,0:T(8,128)}) %reduce-scatter.3.cloned.1.call-update) | async-done | bytes 98320 | tf_op jit(solution)/shard_map/reduce_scatter | solution.py:50
  381.7 3.0 fusion.14
  384.7 0.0 all-reduce.3.cloned.1.call-update
  384.7 0.0 copy-done.1
  384.7 1.6 pad_maximum_fusion.1
  386.3 134.4 %all-reduce.3.cloned.1.call-done = (f32[512,512]{1,0:T(8,128)}, f32[512,512]{1,0:T(8,128)}) async-done(((f32[512,512]{1,0:T(8,128)}, f32[512,512]{1,0:T(8,128)}), (f32[512,512]{1,0:T(8,128)}, f32[512,512]{1,0:T(8,128)})) %all-reduce.3.cloned.1.call-update) | async-done | bytes 2097168 | tf_op jit(solution)/shard_map/psum | solution.py:55
  520.7 2.0 fusion.11
  522.8 1.5 pad_maximum_fusion
  (12 shorter events, 0.0 us)
Async XLA Ops:
  7.2 69.7 %all-gather.7.cloned.1.call-start = ((), (), s32[]{:S(2)}) async-start(), calls=%async_computation.5 | async-start | bytes 3932160 | tf_op jit(solution)/shard_map/all_gather | solution.py:24
  9.9 161.5 %all-gather.5.cloned.1.call-start = ((), (), s32[]{:S(2)}) async-start(), calls=%async_computation.4 | async-start | bytes 3932160 | tf_op jit(solution)/shard_map/all_gather | solution.py:24
  10.6 265.3 %reduce-scatter.5.cloned.1.call-start = ((), (), s32[]{:S(2)}) async-start(), calls=%async_computation.3 | async-start | bytes 3244032 | tf_op jit(solution)/shard_map/reduce_scatter | solution.py:50
  40.8 35.1 %copy-start.10 = (s32[2,6]{1,0:T(2,128)S(1)}, s32[2,6]{1,0:T(2,128)}, u32[]{:S(2)}) copy-start(s32[2,6]{1,0:T(2,128)} %param.7) | copy-start | bytes 148
  76.3 10.9 %copy-start.4 = (s32[6]{0:T(128)}, s32[6]{0:T(128)S(1)}, u32[]{:S(2)}) copy-start(s32[6]{0:T(128)S(1)} %get-tuple-element.9) | copy-start | bytes 76
  76.3 10.9 %copy-start.6 = (s32[8]{0:T(128)}, s32[8]{0:T(128)S(1)}, u32[]{:S(2)}) copy-start(s32[8]{0:T(128)S(1)} %iota_add_fusion) | copy-start | bytes 100
  146.9 10.5 %copy-start.5 = (s32[6]{0:T(128)S(1)}, s32[6]{0:T(128)}, u32[]{:S(2)}) copy-start(s32[6]{0:T(128)} %copy-done.4) | copy-start | bytes 76
  146.9 10.5 %copy-start.8 = (s32[16]{0:T(128)S(1)}, s32[16]{0:T(128)}, u32[]{:S(2)}) copy-start(s32[16]{0:T(128)} %iota_add_fusion.1) | copy-start | bytes 196
  171.3 5.7 %copy-start.2 = (s32[6]{0:T(128)S(1)}, s32[6]{0:T(128)}, u32[]{:S(2)}) copy-start(s32[6]{0:T(128)} %get-tuple-element.8) | copy-start | bytes 76
  171.3 5.7 %copy-start.7 = (s32[8]{0:T(128)S(1)}, s32[8]{0:T(128)}, u32[]{:S(2)}) copy-start(s32[8]{0:T(128)} %copy-done.6) | copy-start | bytes 100
  171.3 210.4 %reduce-scatter.3.cloned.1.call-start = ((), (), s32[]{:S(2)}) async-start(), calls=%async_computation.2 | async-start | bytes 3244032 | tf_op jit(solution)/shard_map/reduce_scatter | solution.py:50
  241.1 10.6 %copy-start.3 = (s32[6]{0:T(128)S(1)}, s32[6]{0:T(128)}, u32[]{:S(2)}) copy-start(s32[6]{0:T(128)} %get-tuple-element.8) | copy-start | bytes 76
  241.1 10.6 %copy-start.9 = (s32[16]{0:T(128)S(1)}, s32[16]{0:T(128)}, u32[]{:S(2)}) copy-start(s32[16]{0:T(128)} %iota_add_fusion.1) | copy-start | bytes 196
  265.7 255.1 %copy-start = (f32[2,512,512]{2,1,0:T(8,128)S(1)}, f32[2,512,512]{2,1,0:T(8,128)}, u32[]{:S(2)}) copy-start(f32[2,512,512]{2,1,0:T(8,128)} %param.6) | copy-start | bytes 6291460
  265.7 255.0 %all-reduce.3.cloned.1.call-start = ((), (), s32[]{:S(2)}) async-start(), calls=%async_computation.6 | async-start | bytes 4194304 | tf_op jit(solution)/shard_map/psum | solution.py:55
  275.9 108.8 %copy-start.1 = (f32[48,512]{1,0:T(8,128)S(1)}, f32[48,512]{1,0:T(8,128)}, u32[]{:S(2)}) copy-start(f32[48,512]{1,0:T(8,128)} %reduce-scatter.5.cloned.1.call-done) | copy-start | bytes 294916
Sparse Core Ops, SparseCore 0:
  10.0 66.1 all-gather.6
  78.4 62.1 all-gather.4
  171.4 104.4 reduce-scatter.4
  281.2 100.4 reduce-scatter.2
  387.7 133.0 all-reduce.2
where the time goes:
time: 538 us; the launch traced here: 531 us
  waiting for transfers between devices  248 us (46%)
  matrix products  151 us (28%)
  local copies, waits for them, and re-layouts  111 us (21%)
  between operations  14.4 us (3%)
  other arithmetic  5.61 us (1%)
    psum x1, waiting for transfers between devices, per_device(): summed = lax.psum(term, ('prow', 'pcol'))  134 us
    dot_general x2, matrix products, per_device(): jnp.einsum('aibj,bjw->aiw', grid_tiles, picked, precision=highest, prefer...  119 us
    reduce_scatter x2, waiting for transfers between devices, per_device(): lax.psum_scatter(partial_sum, ('prow', 'pcol'), scatter_dimension=0, tile...  113 us
    unnamed x25, local copies, waits for them, and re-layouts  51.2 us
    reshape x1, local copies, waits for them, and re-layouts, per_device(): grid_tiles = ancestor_inv.reshape(tile_rows, TILE, tile_cols, TILE)  35.1 us
    dot_general x2, matrix products, per_device(): jnp.dot(pick_row, products.reshape(tile_rows, TILE * W), precision=highes...  17 us
    reshape x2, local copies, waits for them, and re-layouts, per_device(): lfull.reshape(NS, TILE * W)  11.2 us
    reshape x2, local copies, waits for them, and re-layouts, per_device(): partial_sum = partial_sum.reshape(total_rows, W)  10.9 us
  transfers between devices with their start and end apart: 5, of which 3 were waited for; matrix products, arithmetic and copies ran while one was open for 49% of the time, Pallas kernels for 0%

commit v1 on v0

v1 whole, which is shorter than its diff:
```python
import functools

import jax
import jax.numpy as jnp
from jax import lax
from jax.experimental import pallas as pl
from jax.experimental.pallas import tpu as pltpu
from jax.sharding import PartitionSpec as P

TILE = 256
W = 512
NS = 6
NSUP = 2
MESH = pl.DeviceIdType.MESH


def place(stage):
    row = lax.axis_index("prow")
    col = lax.axis_index("pcol")
    core = lax.rem(col, 2)
    chip = col // 2
    if stage == "row":
        return row, lambda m: (m, col)
    if stage == "chip":
        return chip, lambda m: (row, m * 2 + core)
    return core, lambda m: (row, chip * 2 + m)


def exchange_kernel(stage, size, scatter, x_ref, out_ref, send_sem, recv_sem, own_sem):
    me, device = place(stage)
    barrier = pltpu.get_barrier_semaphore()
    for step in range(1, size):
        pl.semaphore_signal(
            barrier, inc=1, device_id=device(lax.rem(me + step, size)), device_id_type=MESH
        )
    pl.semaphore_wait(barrier, size - 1)
    copies = []
    for step in range(1, size):
        to = lax.rem(me + step, size)
        copy = pltpu.make_async_remote_copy(
            src_ref=x_ref.at[to] if scatter else x_ref,
            dst_ref=out_ref.at[me],
            send_sem=send_sem.at[step - 1],
            recv_sem=recv_sem.at[step - 1],
            device_id=device(to),
            device_id_type=MESH,
        )
        copy.start()
        copies.append(copy)
    own = pltpu.make_async_copy(x_ref.at[me] if scatter else x_ref, out_ref.at[me], own_sem)
    own.start()
    own.wait()
    for copy in copies:
        copy.wait()


def exchange(x, stage, size, scatter, collective_id):
    shape = x.shape if scatter else (size,) + x.shape
    return pl.pallas_call(
        functools.partial(exchange_kernel, stage, size, scatter),
        out_shape=jax.ShapeDtypeStruct(shape, x.dtype),
        in_specs=[pl.BlockSpec(memory_space=pl.ANY)],
        out_specs=pl.BlockSpec(memory_space=pl.ANY),
        scratch_shapes=[
            pltpu.SemaphoreType.DMA((size - 1,)),
            pltpu.SemaphoreType.DMA((size - 1,)),
            pltpu.SemaphoreType.DMA,
        ],
        compiler_params=pltpu.CompilerParams(
            collective_id=collective_id, has_side_effects=True
        ),
    )(x)


def product_kernel(rows_ref, cols_ref, a_ref, l_ref, p_ref, d_ref):
    sup, i, j = pl.program_id(0), pl.program_id(1), pl.program_id(2)
    highest = lax.Precision.HIGHEST
    row_hit = rows_ref[sup, i] >= 0

    @pl.when((i == 0) & (j == 0))
    def _():
        d_ref[...] = jnp.zeros_like(d_ref)

    @pl.when(j == 0)
    def _():
        p_ref[...] = jnp.zeros_like(p_ref)

    @pl.when(row_hit & (cols_ref[sup, j] >= 0))
    def _():
        block = l_ref[0, pl.ds(pl.multiple_of(j * TILE, TILE), TILE), :]
        p_ref[0] -= jnp.dot(
            a_ref[...], block, precision=highest, preferred_element_type=jnp.float32
        )

    @pl.when(row_hit & (j == NS - 1))
    def _():
        block = l_ref[0, pl.ds(pl.multiple_of(i * TILE, TILE), TILE), :]
        d_ref[0] += lax.dot_general(
            block,
            p_ref[0],
            (((0,), (0,)), ((), ())),
            precision=highest,
            preferred_element_type=jnp.float32,
        )


def products(rows, cols, ancestor, lfull):
    def a_map(sup, i, j, rows_ref, cols_ref):
        row, col = rows_ref[sup, i], cols_ref[sup, j]
        hit = (row >= 0) & (col >= 0)
        return jnp.where(hit, row, 0), jnp.where(hit, col, 0)

    total = lfull.shape[1]
    return pl.pallas_call(
        product_kernel,
        out_shape=(
            jax.ShapeDtypeStruct((NSUP, total, W), jnp.float32),
            jax.ShapeDtypeStruct((NSUP, W, W), jnp.float32),
        ),
        grid_spec=pltpu.PrefetchScalarGridSpec(
            num_scalar_prefetch=2,
            grid=(NSUP, NS, NS),
            in_specs=[
                pl.BlockSpec((TILE, TILE), a_map),
                pl.BlockSpec((1, total, W), lambda sup, i, j, *_: (sup, 0, 0)),
            ],
            out_specs=[
                pl.BlockSpec((1, TILE, W), lambda sup, i, j, *_: (sup, i, 0)),
                pl.BlockSpec((1, W, W), lambda sup, i, j, *_: (sup, 0, 0)),
            ],
        ),
        compiler_params=pltpu.CompilerParams(vmem_limit_bytes=40 * 1024 * 1024),
    )(rows, cols, ancestor, lfull)


def per_device(nrow, ncol, ancestor_inv, l_scaled, diag_inv, tile_lists):
    nchip = ncol // 2
    tile_rows = ancestor_inv.shape[0] // TILE
    tile_cols = ancestor_inv.shape[1] // TILE
    row_pos = lax.axis_index("prow")
    col_pos = lax.axis_index("pcol")
    count = l_scaled.shape[1] // ncol
    part = W // (nrow * ncol)
    total = l_scaled.shape[1] * nrow

    share = lax.dynamic_slice_in_dim(l_scaled, col_pos * count, count, 1)
    held = exchange(share, "row", nrow, False, 1)
    held = exchange(held, "chip", nchip, False, 2)
    held = exchange(held, "core", 2, False, 3)
    lfull = held.transpose(3, 2, 1, 0, 4, 5).reshape(NSUP, total, W)

    rows = tile_lists - row_pos * tile_rows
    rows = jnp.where((rows >= 0) & (rows < tile_rows), rows, -1)
    cols = tile_lists - col_pos * tile_cols
    cols = jnp.where((cols >= 0) & (cols < tile_cols), cols, -1)
    partial, terms = products(rows, cols, ancestor_inv, lfull)

    partial = partial.reshape(NSUP, nrow, nchip, 2, count, W)
    terms = terms.reshape(NSUP, nrow, nchip, 2, part, W)
    sums = jnp.concatenate([partial, terms], axis=4).transpose(3, 2, 1, 0, 4, 5)
    sums = exchange(sums, "core", 2, True, 4).sum(0)
    sums = exchange(sums, "chip", nchip, True, 5).sum(0)
    sums = exchange(sums, "row", nrow, True, 6).sum(0)
    mine = sums[:, :count]

    diag = exchange(sums[:, count:], "row", nrow, False, 7)
    diag = exchange(diag, "chip", nchip, False, 8)
    diag = exchange(diag, "core", 2, False, 9)
    diag = diag.transpose(3, 2, 1, 0, 4, 5).reshape(NSUP, W, W)
    return mine, diag_inv - diag


def solution(mesh):
    placed = (P("prow", "pcol"), P(None, "prow", None), P(), P())
    return jax.shard_map(
        functools.partial(per_device, mesh.shape["prow"], mesh.shape["pcol"]),
        mesh=mesh,
        in_specs=placed,
        out_specs=(P(None, ("prow", "pcol"), None), P()),
        check_vma=False,
    )
```

time: 538 us -> 471 us (0.88); the launches traced: 531 us -> 475 us
  Pallas kernels: 0 us -> 443 us
  waiting for transfers between devices: 248 us -> 0 us
  matrix products: 151 us -> 0 us
  local copies, waits for them, and re-layouts: 111 us -> 11.3 us
  other arithmetic: 5.61 us -> 19.9 us
  between operations: 14.4 us -> 0.74 us
    pallas_call x0 -> x10, Pallas kernels: none -> 443 us  [the longest x9 428 us: exchange(): pl.pallas_call(functools.partial(exchange_kernel, stage, size, scatter),...]
    dot_general x8 -> x0, matrix products: 151 us -> none  [the longest x2 119 us: per_device(): jnp.einsum('aibj,bjw->aiw', grid_tiles, picked, precision=highest, prefer...]
    psum x1 -> x0, waiting for transfers between devices: 134 us -> none  [per_device(): summed = lax.psum(term, ('prow', 'pcol'))]
    reduce_scatter x2 -> x0, waiting for transfers between devices: 113 us -> none  [per_device(): lax.psum_scatter(partial_sum, ('prow', 'pcol'), scatter_dimension=0, tile...]
    reshape x5 -> x0, local copies, waits for them, and re-layouts: 57.1 us -> none  [the longest x1 35.1 us: per_device(): grid_tiles = ancestor_inv.reshape(tile_rows, TILE, tile_cols, TILE)]
    unnamed x25 -> x4, local copies, waits for them, and re-layouts: 51.2 us -> 0.62 us
    reduce_sum x0 -> x3, other arithmetic: none -> 11.9 us  [the longest x1 6.81 us: per_device(): sums = exchange(sums, 'core', 2, True, 4).sum(0)]
    transpose x0 -> x2, local copies, waits for them, and re-layouts: none -> 8.63 us  [the longest x1 6.75 us: per_device(): lfull = held.transpose(3, 2, 1, 0, 4, 5).reshape(NSUP, total, W)]
  transfers between devices with their start and end apart: 5 -> 0, of which waited for: 3 -> 0; matrix products, arithmetic and copies ran while one was open for 49% -> 0% of each run, Pallas kernels for 0% -> 0%
where the time goes in v1:
time: 471 us; the launch traced here: 475 us
  Pallas kernels  443 us (94%)
  other arithmetic  19.9 us (4%)
  local copies, waits for them, and re-layouts  11.3 us (2%)
    pallas_call x9, Pallas kernels, exchange(): pl.pallas_call(functools.partial(exchange_kernel, stage, size, scatter),...  428 us
    pallas_call x1, Pallas kernels, products(): pl.pallas_call(product_kernel, out_shape=(jax.ShapeDtypeStruct((NSUP, tot...  15.2 us

profile of v1, /device:TPU:0, one launch (start us, length us, event | category | flops | bytes accessed | tf_op | source)
XLA Modules:
  0.0 474.9 jit_solution(10245923684750691851)
XLA Ops:
  0.6 0.0 copy-start
  0.7 0.8 and_select_fusion
  1.5 0.6 copy-done
  2.1 0.7 constant_dynamic-slice_fusion.x_ref
  2.8 19.1 %shard_map.59.x_ref = f32[4,2,48,512]{3,2,1,0:T(8,128)} custom-call(f32[2,48,512]{2,1,0:T(8,128)} %constant_dynamic-slice_fusion.x_ref), custom_call_target="tpu_custom_call" | custom-call | tf_op jit(solution)/shard_map/pallas_call | solution.py:59
  21.8 37.7 %shard_map.60.x_ref = f32[4,4,2,48,512]{4,3,2,1,0:T(8,128)} custom-call(f32[4,2,48,512]{3,2,1,0:T(8,128)} %shard_map.59.x_ref), custom_call_target="tpu_custom_call" | custom-call | tf_op jit(solution)/shard_map/pallas_call | solution.py:59
  59.5 96.4 %shard_map.61 = f32[2,4,4,2,48,512]{5,4,3,2,1,0:T(8,128)} custom-call(f32[4,4,2,48,512]{4,3,2,1,0:T(8,128)} %shard_map.60.x_ref), custom_call_target="tpu_custom_call" | custom-call | tf_op jit(solution)/shard_map/pallas_call | solution.py:59
  155.9 6.7 %copy.7 = f32[2,4,4,2,48,512]{5,4,3,2,1,0:T(8,128)} copy(f32[2,4,4,2,48,512]{5,4,0,1,2,3:T(8,128)} %bitcast.12) | data formatting | bytes 12582912 | tf_op jit(solution)/shard_map/transpose | solution.py:150
  162.7 15.2 %shard_map.62 = (f32[2,1536,512]{2,1,0:T(8,128)S(1)}, f32[2,512,512]{2,1,0:T(8,128)S(1)}) custom-call(s32[2,6]{1,0:T(2,128)S(1)} %get-tuple-element.7.rows_ref, s32[2,6]{1,0:T(2,128)S(1)} %get-tuple-element.6.cols_ref, f32[4096,2048]{1,0:T(8,128)} %a_ref.1, f32[2,1536,512]{2,1,0:T(8,128)} %bitcast.11), custom_call_target="tpu_custom_call" | custom-call | tf_op jit(solution)/shard_map/pallas_call | solution.py:114
  177.9 3.9 copy_bitcast_fusion.x_ref
  181.9 129.5 %shard_map.63 = f32[2,4,4,2,64,512]{5,4,3,2,1,0:T(8,128)} custom-call(f32[2,4,4,2,64,512]{5,4,3,2,1,0:T(8,128)} %copy_bitcast_fusion.x_ref), custom_call_target="tpu_custom_call" | custom-call | tf_op jit(solution)/shard_map/pallas_call | solution.py:59
  311.4 6.8 %reduce_sum.27.x_ref = f32[4,4,2,64,512]{4,3,2,1,0:T(8,128)} reduce(f32[2,4,4,2,64,512]{5,4,3,2,1,0:T(8,128)} %shard_map.63, f32[]{:T(128)} %constant.7.clone.1), dimensions={0}, to_apply=%region_0.1 | reduce | flops 1048576 | bytes 12582916 | tf_op jit(solution)/shard_map/reduce_sum | solution.py:161
  318.2 54.3 %shard_map.64 = f32[4,4,2,64,512]{4,3,2,1,0:T(8,128)} custom-call(f32[4,4,2,64,512]{4,3,2,1,0:T(8,128)} %reduce_sum.27.x_ref), custom_call_target="tpu_custom_call" | custom-call | tf_op jit(solution)/shard_map/pallas_call | solution.py:59
  372.5 3.8 reduce_sum.28.x_ref
  376.3 30.1 %shard_map.65 = f32[4,2,64,512]{3,2,1,0:T(8,128)} custom-call(f32[4,2,64,512]{3,2,1,0:T(8,128)} %reduce_sum.28.x_ref), custom_call_target="tpu_custom_call" | custom-call | tf_op jit(solution)/shard_map/pallas_call | solution.py:59
  406.4 1.3 reduce_sum.29
  407.8 0.6 slice.9.x_ref
  408.4 0.7 slice.8
  409.1 13.5 %shard_map.66.x_ref = f32[4,2,16,512]{3,2,1,0:T(8,128)} custom-call(f32[2,16,512]{2,1,0:T(8,128)} %slice.9.x_ref), custom_call_target="tpu_custom_call" | custom-call | tf_op jit(solution)/shard_map/pallas_call | solution.py:59
  422.6 14.3 %shard_map.67.x_ref = f32[4,4,2,16,512]{4,3,2,1,0:T(8,128)} custom-call(f32[4,2,16,512]{3,2,1,0:T(8,128)} %shard_map.66.x_ref), custom_call_target="tpu_custom_call" | custom-call | tf_op jit(solution)/shard_map/pallas_call | solution.py:59
  436.8 32.9 %shard_map.68 = f32[2,4,4,2,16,512]{5,4,3,2,1,0:T(8,128)} custom-call(f32[4,4,2,16,512]{4,3,2,1,0:T(8,128)} %shard_map.67.x_ref), custom_call_target="tpu_custom_call" | custom-call | tf_op jit(solution)/shard_map/pallas_call | solution.py:59
  469.8 0.0 copy-start.1
  469.8 1.9 copy.10
  471.7 3.2 bitcast_subtract_fusion
  474.9 0.0 copy-done.1
Async XLA Ops:
  0.6 1.4 copy-start
  469.8 5.1 %copy-start.1 = (f32[2,384,512]{2,1,0:T(8,128)S(1)}, f32[2,384,512]{2,1,0:T(8,128)}, u32[]{:S(2)}) copy-start(f32[2,384,512]{2,1,0:T(8,128)} %param.5) | copy-start | bytes 4718596

commit v2 on v1

--- a/solution.py
+++ b/solution.py
@@ -26,7 +26,7 @@
     return core, lambda m: (row, chip * 2 + m)
 
 
-def exchange_kernel(stage, size, scatter, x_ref, out_ref, send_sem, recv_sem, own_sem):
+def exchange_kernel(stage, size, scatter, x_ref, out_ref, send_sem, recv_sem):
     me, device = place(stage)
     barrier = pltpu.get_barrier_semaphore()
     for step in range(1, size):
@@ -47,16 +47,13 @@
         )
         copy.start()
         copies.append(copy)
-    own = pltpu.make_async_copy(x_ref.at[me] if scatter else x_ref, out_ref.at[me], own_sem)
-    own.start()
-    own.wait()
     for copy in copies:
         copy.wait()
 
 
 def exchange(x, stage, size, scatter, collective_id):
     shape = x.shape if scatter else (size,) + x.shape
-    return pl.pallas_call(
+    moved = pl.pallas_call(
         functools.partial(exchange_kernel, stage, size, scatter),
         out_shape=jax.ShapeDtypeStruct(shape, x.dtype),
         in_specs=[pl.BlockSpec(memory_space=pl.ANY)],
@@ -64,12 +61,18 @@
         scratch_shapes=[
             pltpu.SemaphoreType.DMA((size - 1,)),
             pltpu.SemaphoreType.DMA((size - 1,)),
-            pltpu.SemaphoreType.DMA,
         ],
         compiler_params=pltpu.CompilerParams(
             collective_id=collective_id, has_side_effects=True
         ),
     )(x)
+    me, _ = place(stage)
+    if not scatter:
+        return lax.dynamic_update_index_in_dim(moved, x, me, 0)
+    own = lax.dynamic_index_in_dim(x, me, 0, keepdims=False)
+    for step in range(1, size):
+        own += lax.dynamic_index_in_dim(moved, lax.rem(me + step, size), 0, keepdims=False)
+    return own
 
 
 def product_kernel(rows_ref, cols_ref, a_ref, l_ref, p_ref, d_ref):
@@ -158,9 +161,9 @@
     partial = partial.reshape(NSUP, nrow, nchip, 2, count, W)
     terms = terms.reshape(NSUP, nrow, nchip, 2, part, W)
     sums = jnp.concatenate([partial, terms], axis=4).transpose(3, 2, 1, 0, 4, 5)
-    sums = exchange(sums, "core", 2, True, 4).sum(0)
-    sums = exchange(sums, "chip", nchip, True, 5).sum(0)
-    sums = exchange(sums, "row", nrow, True, 6).sum(0)
+    sums = exchange(sums, "core", 2, True, 4)
+    sums = exchange(sums, "chip", nchip, True, 5)
+    sums = exchange(sums, "row", nrow, True, 6)
     mine = sums[:, :count]
 
     diag = exchange(sums[:, count:], "row", nrow, False, 7)

time: 471 us -> 240 us (0.51)
  Pallas kernels: 443 us -> 199 us
  local copies, waits for them, and re-layouts: 11.3 us -> 20.7 us
    pallas_call x9, Pallas kernels: 428 us -> 180 us  [exchange(): pl.pallas_call(functools.partial(exchange_kernel, stage, size, scatter),...]
    reduce_sum x3 -> x0, other arithmetic: 11.9 us -> none  [the longest x1 6.81 us: per_device(): sums = exchange(sums, 'core', 2, True, 4).sum(0)]
    add x0 -> x3, other arithmetic: none -> 11.7 us  [exchange(): own += lax.dynamic_index_in_dim(moved, lax.rem(me + step, size), 0, keepd...]
    dynamic_update_slice x0 -> x6, local copies, waits for them, and re-layouts: none -> 9.27 us  [exchange(): return lax.dynamic_update_index_in_dim(moved, x, me, 0)]
    concatenate x0 -> x1, other arithmetic: none -> 7.31 us  [per_device(): sums = jnp.concatenate([partial, terms], axis=4).transpose(3, 2, 1, 0, 4, 5)]
where the time goes in v2:
time: 240 us; the launch traced here: 242 us
  Pallas kernels  199 us (83%)
  other arithmetic  20.8 us (9%)
  local copies, waits for them, and re-layouts  20.7 us (9%)
    pallas_call x9, Pallas kernels, exchange(): pl.pallas_call(functools.partial(exchange_kernel, stage, size, scatter),...  180 us
    pallas_call x1, Pallas kernels, products(): pl.pallas_call(product_kernel, out_shape=(jax.ShapeDtypeStruct((NSUP, tot...  19.7 us
    add x3, other arithmetic, exchange(): own += lax.dynamic_index_in_dim(moved, lax.rem(me + step, size), 0, keepd...  11.7 us
    dynamic_update_slice x6, local copies, waits for them, and re-layouts, exchange(): return lax.dynamic_update_index_in_dim(moved, x, me, 0)  9.27 us
    concatenate x1, other arithmetic, per_device(): sums = jnp.concatenate([partial, terms], axis=4).transpose(3, 2, 1, 0, 4, 5)  7.31 us
    transpose x1, local copies, waits for them, and re-layouts, per_device(): lfull = held.transpose(3, 2, 1, 0, 4, 5).reshape(NSUP, total, W)  6.74 us

profile of v2, /device:TPU:0, one launch (start us, length us, event | category | flops | bytes accessed | tf_op | source)
XLA Modules:
  0.0 241.7 jit_solution(7120109340903896592)
XLA Ops:
  0.7 1.6 constant_dynamic-slice_fusion.x_ref
  2.3 19.0 %shard_map.59 = f32[4,2,48,512]{3,2,1,0:T(8,128)} custom-call(f32[2,48,512]{2,1,0:T(8,128)} %constant_dynamic-slice_fusion.x_ref), custom_call_target="tpu_custom_call" | custom-call | tf_op jit(solution)/shard_map/pallas_call | solution.py:56
  21.3 1.6 bitcast_dynamic-update-slice_fusion.4.x_ref
  23.0 0.0 copy-start.1
  23.0 37.6 %shard_map.60 = f32[4,4,2,48,512]{4,3,2,1,0:T(8,128)} custom-call(f32[4,2,48,512]{3,2,1,0:T(8,128)} %bitcast_dynamic-update-slice_fusion.4.x_ref), custom_call_target="tpu_custom_call" | custom-call | tf_op jit(solution)/shard_map/pallas_call | solution.py:56
  60.6 0.0 copy-done.1
  60.6 1.0 bitcast_dynamic-update-slice_fusion.2.x_ref
  61.6 0.0 copy-start
  61.6 6.0 %shard_map.61 = f32[2,4,4,2,48,512]{5,4,3,2,1,0:T(8,128)} custom-call(f32[4,4,2,48,512]{4,3,2,1,0:T(8,128)} %bitcast_dynamic-update-slice_fusion.2.x_ref), custom_call_target="tpu_custom_call" | custom-call | tf_op jit(solution)/shard_map/pallas_call | solution.py:56
  67.6 0.0 copy-done
  67.6 2.0 bitcast_dynamic-update-slice_fusion
  69.7 0.0 copy-start.3
  69.7 6.7 %copy.7 = f32[2,4,4,2,48,512]{5,4,3,2,1,0:T(8,128)} copy(f32[2,4,4,2,48,512]{5,4,0,1,2,3:T(8,128)} %bitcast.44) | data formatting | bytes 12582912 | tf_op jit(solution)/shard_map/transpose | solution.py:153
  76.4 0.0 copy-done.3
  76.4 19.7 %shard_map.62 = (f32[2,1536,512]{2,1,0:T(8,128)S(1)}, f32[2,512,512]{2,1,0:T(8,128)S(1)}) custom-call(s32[2,6]{1,0:T(2,128)S(1)} %get-tuple-element.9.rows_ref, s32[2,6]{1,0:T(2,128)S(1)} %get-tuple-element.8.cols_ref, f32[4096,2048]{1,0:T(8,128)} %a_ref.1, f32[2,1536,512]{2,1,0:T(8,128)} %bitcast.43), custom_call_target="tpu_custom_call" | custom-call | tf_op jit(solution)/shard_map/pallas_call | solution.py:117
  96.1 7.3 %fusion.5 = (f32[2,4,4,2,64,512]{5,4,0,1,2,3:T(8,128)}, f32[2,4,4,2,64,512]{5,4,3,2,1,0:T(8,128)}) fusion(f32[2,4,4,2,16,512]{5,4,3,2,1,0:T(8,128)S(1)} %bitcast.42, f32[2,4,4,2,48,512]{5,4,3,2,1,0:T(8,128)S(1)} %bitcast.41), kind=kLoop, calls=%fused_computation.20 | loop fusion | flops 2097152 | bytes 25165824 | tf_op jit(solution)/shard_map/concatenate | solution.py:163
  103.5 7.5 %shard_map.63 = f32[2,4,4,2,64,512]{5,4,3,2,1,0:T(8,128)} custom-call(f32[2,4,4,2,64,512]{5,4,3,2,1,0:T(8,128)} %get-tuple-element.7.x_ref), custom_call_target="tpu_custom_call" | custom-call | tf_op jit(solution)/shard_map/pallas_call | solution.py:56
  111.0 6.8 %bitcast_add_fusion = f32[1,4,4,2,64,512]{5,4,3,2,1,0:T(8,128)} fusion(f32[2,4,4,2,64,512]{5,4,3,2,1,0:T(8,128)} %shard_map.63, s32[]{:T(128)S(6)} %select_n.69, f32[2,4,4,2,64,512]{5,4,0,1,2,3:T(8,128)} %get-tuple-element.6, s32[]{:T(128)S(6)} %select_n.68), kind=kLoop, calls=%fused_computation.1 | loop fusion | flops 1048576 | bytes 12582920 | tf_op jit(solution)/shard_map/add | solution.py:74
  117.7 48.5 %shard_map.64 = f32[4,4,2,64,512]{4,3,2,1,0:T(8,128)} custom-call(f32[4,4,2,64,512]{4,3,2,1,0:T(8,128)} %bitcast.45), custom_call_target="tpu_custom_call" | custom-call | tf_op jit(solution)/shard_map/pallas_call | solution.py:56
  166.3 3.6 %fusion.1 = f32[1,4,2,64,512]{4,3,2,1,0:T(8,128)} fusion(f32[4,4,2,64,512]{4,3,2,1,0:T(8,128)} %shard_map.64, s32[]{:T(128)S(6)} %select_n.72, s32[]{:T(128)S(6)} %select_n.71, s32[]{:T(128)S(6)} %select_n.70, f32[1,4,4,2,64,512]{5,4,3,2,1,0:T(8,128)} %bitcast_add_fusion, s32[]{:T(128)S(6)} %select_n.67), kind=kLoop, calls=%fused_computation.7 | loop fusion | flops 786432 | bytes 5242896 | tf_op jit(solution)/shard_map/add | solution.py:74
  169.9 30.2 %shard_map.65 = f32[4,2,64,512]{3,2,1,0:T(8,128)} custom-call(f32[4,2,64,512]{3,2,1,0:T(8,128)} %bitcast.47), custom_call_target="tpu_custom_call" | custom-call | tf_op jit(solution)/shard_map/pallas_call | solution.py:56
  200.1 1.3 fusion.4
  201.4 0.6 slice.9.x_ref
  202.0 13.5 %shard_map.66 = f32[4,2,16,512]{3,2,1,0:T(8,128)} custom-call(f32[2,16,512]{2,1,0:T(8,128)} %slice.9.x_ref), custom_call_target="tpu_custom_call" | custom-call | tf_op jit(solution)/shard_map/pallas_call | solution.py:56
  215.5 0.6 bitcast_dynamic-update-slice_fusion.5.x_ref
  216.1 14.2 %shard_map.67 = f32[4,4,2,16,512]{4,3,2,1,0:T(8,128)} custom-call(f32[4,2,16,512]{3,2,1,0:T(8,128)} %bitcast_dynamic-update-slice_fusion.5.x_ref), custom_call_target="tpu_custom_call" | custom-call | tf_op jit(solution)/shard_map/pallas_call | solution.py:56
  230.4 1.7 bitcast_dynamic-update-slice_fusion.3.x_ref
  232.1 0.0 copy-start.2
  232.1 3.0 %shard_map.68 = f32[2,4,4,2,16,512]{5,4,3,2,1,0:T(8,128)} custom-call(f32[4,4,2,16,512]{4,3,2,1,0:T(8,128)} %bitcast_dynamic-update-slice_fusion.3.x_ref), custom_call_target="tpu_custom_call" | custom-call | tf_op jit(solution)/shard_map/pallas_call | solution.py:56
  235.1 2.3 bitcast_dynamic-update-slice_fusion.1
  237.4 1.8 copy.10
  239.2 0.0 copy-done.2
  239.2 1.8 bitcast_subtract_fusion
  241.0 0.7 slice.8
  (1 shorter events, 0.0 us)
Async XLA Ops:
  23.0 37.6 %copy-start.1 = (f32[4,2,48,512]{3,2,1,0:T(8,128)S(1)}, f32[4,2,48,512]{3,2,1,0:T(8,128)}, u32[]{:S(2)}) copy-start(f32[4,2,48,512]{3,2,1,0:T(8,128)} %bitcast_dynamic-update-slice_fusion.4.x_ref) | copy-start | bytes 2359300
  61.6 6.0 %copy-start = (f32[4,4,2,48,512]{4,3,2,1,0:T(8,128)S(1)}, f32[4,4,2,48,512]{4,3,2,1,0:T(8,128)}, u32[]{:S(2)}) copy-start(f32[4,4,2,48,512]{4,3,2,1,0:T(8,128)} %bitcast_dynamic-update-slice_fusion.2.x_ref) | copy-start | bytes 9437188
  69.7 6.7 %copy-start.3 = (s32[2,6]{1,0:T(2,128)S(1)}, s32[2,6]{1,0:T(2,128)}, u32[]{:S(2)}) copy-start(s32[2,6]{1,0:T(2,128)} %param.7) | copy-start | bytes 148
  232.1 7.1 %copy-start.2 = (f32[2,512,512]{2,1,0:T(8,128)S(1)}, f32[2,512,512]{2,1,0:T(8,128)}, u32[]{:S(2)}) copy-start(f32[2,512,512]{2,1,0:T(8,128)} %param.6) | copy-start | bytes 6291460

commit v3 on v1

--- a/solution.py
+++ b/solution.py
@@ -26,50 +26,142 @@
     return core, lambda m: (row, chip * 2 + m)
 
 
-def exchange_kernel(stage, size, scatter, x_ref, out_ref, send_sem, recv_sem, own_sem):
+def enter(peers):
+    barrier = pltpu.get_barrier_semaphore()
+    for peer in peers:
+        pl.semaphore_signal(barrier, inc=1, device_id=peer, device_id_type=MESH)
+    pl.semaphore_wait(barrier, len(peers))
+
+
+def others(stage, size):
     me, device = place(stage)
-    barrier = pltpu.get_barrier_semaphore()
-    for step in range(1, size):
-        pl.semaphore_signal(
-            barrier, inc=1, device_id=device(lax.rem(me + step, size)), device_id_type=MESH
-        )
-    pl.semaphore_wait(barrier, size - 1)
+    return [device(lax.rem(me + step, size)) for step in range(1, size)]
+
+
+def scatter_kernel(stage, size, axis, x_ref, y_ref, x_out, y_out, send_sem, recv_sem):
+    me, _ = place(stage)
+    peers = others(stage, size)
+    enter(peers)
     copies = []
-    for step in range(1, size):
-        to = lax.rem(me + step, size)
-        copy = pltpu.make_async_remote_copy(
-            src_ref=x_ref.at[to] if scatter else x_ref,
-            dst_ref=out_ref.at[me],
-            send_sem=send_sem.at[step - 1],
-            recv_sem=recv_sem.at[step - 1],
-            device_id=device(to),
-            device_id_type=MESH,
-        )
-        copy.start()
-        copies.append(copy)
-    own = pltpu.make_async_copy(x_ref.at[me] if scatter else x_ref, out_ref.at[me], own_sem)
-    own.start()
-    own.wait()
+    lead = (slice(None),) * axis
+    for step, peer in enumerate(peers):
+        to = lax.rem(me + step + 1, size)
+        for which, (src, dst) in enumerate(((x_ref, x_out), (y_ref, y_out))):
+            copy = pltpu.make_async_remote_copy(
+                src_ref=src.at[lead + (to,)],
+                dst_ref=dst.at[step],
+                send_sem=send_sem.at[step, which],
+                recv_sem=recv_sem.at[step, which],
+                device_id=peer,
+                device_id_type=MESH,
+            )
+            copy.start()
+            copies.append(copy)
     for copy in copies:
         copy.wait()
 
 
-def exchange(x, stage, size, scatter, collective_id):
-    shape = x.shape if scatter else (size,) + x.shape
-    return pl.pallas_call(
-        functools.partial(exchange_kernel, stage, size, scatter),
+def scatter(pair, stage, size, axis, collective_id):
+    shapes = [(size - 1,) + x.shape[:axis] + x.shape[axis + 1:] for x in pair]
+    moved = pl.pallas_call(
+        functools.partial(scatter_kernel, stage, size, axis),
+        out_shape=[jax.ShapeDtypeStruct(shape, jnp.float32) for shape in shapes],
+        in_specs=[pl.BlockSpec(memory_space=pl.ANY)] * 2,
+        out_specs=[pl.BlockSpec(memory_space=pl.ANY)] * 2,
+        scratch_shapes=[
+            pltpu.SemaphoreType.DMA((size - 1, 2)),
+            pltpu.SemaphoreType.DMA((size - 1, 2)),
+        ],
+        compiler_params=pltpu.CompilerParams(
+            collective_id=collective_id, has_side_effects=True
+        ),
+    )(*pair)
+    me, _ = place(stage)
+    sums = []
+    for x, parts in zip(pair, moved):
+        own = lax.dynamic_index_in_dim(x, me, axis, keepdims=False)
+        for step in range(size - 1):
+            own += parts[step]
+        sums.append(own)
+    return sums
+
+
+def gather_kernel(nrow, nchip, x_ref, out_ref, *sems):
+    row_send, row_recv, chip_send, chip_recv, core_send, core_recv = sems
+    row, _ = place("row")
+    chip, _ = place("chip")
+    core, _ = place("core")
+    rows, chips, cores = others("row", nrow), others("chip", nchip), others("core", 2)
+    enter(rows + chips + cores)
+    started = []
+
+    def send(src, slot, send_sem, recv_sem, peer):
+        copy = pltpu.make_async_remote_copy(
+            src_ref=src,
+            dst_ref=slot,
+            send_sem=send_sem,
+            recv_sem=recv_sem,
+            device_id=peer,
+            device_id_type=MESH,
+        )
+        copy.start()
+        started.append(copy)
+        return copy
+
+    mine = out_ref.at[:, row, chip, core]
+    from_rows = [
+        send(x_ref, mine, row_send.at[step], row_recv.at[step], peer)
+        for step, peer in enumerate(rows)
+    ]
+    from_chips = []
+    last = []
+    for near in range(nrow):
+        src = x_ref
+        slot = mine
+        if near > 0:
+            from_rows[near - 1].wait_recv()
+            slot = out_ref.at[:, lax.rem(row - near + nrow, nrow), chip, core]
+            src = slot
+        for step, peer in enumerate(chips):
+            from_chips.append(
+                (
+                    near,
+                    step + 1,
+                    send(src, slot, chip_send.at[step, near], chip_recv.at[step, near], peer),
+                )
+            )
+        last.append(send(src, slot, core_send.at[0, near], core_recv.at[0, near], cores[0]))
+    for near, step, copy in from_chips:
+        copy.wait_recv()
+        slot = out_ref.at[
+            :, lax.rem(row - near + nrow, nrow), lax.rem(chip - step + nchip, nchip), core
+        ]
+        last.append(
+            send(slot, slot, core_send.at[step, near], core_recv.at[step, near], cores[0])
+        )
+    for copy in last:
+        copy.wait_recv()
+    for copy in started:
+        copy.wait_send()
+
+
+def gather(x, nrow, nchip, collective_id):
+    shape = (x.shape[0], nrow, nchip, 2) + x.shape[1:]
+    row, chip, core = ((nrow - 1,), (nchip - 1, nrow), (nchip, nrow))
+    full = pl.pallas_call(
+        functools.partial(gather_kernel, nrow, nchip),
         out_shape=jax.ShapeDtypeStruct(shape, x.dtype),
         in_specs=[pl.BlockSpec(memory_space=pl.ANY)],
         out_specs=pl.BlockSpec(memory_space=pl.ANY),
         scratch_shapes=[
-            pltpu.SemaphoreType.DMA((size - 1,)),
-            pltpu.SemaphoreType.DMA((size - 1,)),
-            pltpu.SemaphoreType.DMA,
+            pltpu.SemaphoreType.DMA(n) for n in (row, row, chip, chip, core, core)
         ],
         compiler_params=pltpu.CompilerParams(
             collective_id=collective_id, has_side_effects=True
         ),
     )(x)
+    where = (0, place("row")[0], place("chip")[0], place("core")[0], 0, 0)
+    return lax.dynamic_update_slice(full, x[:, None, None, None], where)
 
 
 def product_kernel(rows_ref, cols_ref, a_ref, l_ref, p_ref, d_ref):
@@ -144,29 +236,23 @@
     total = l_scaled.shape[1] * nrow
 
     share = lax.dynamic_slice_in_dim(l_scaled, col_pos * count, count, 1)
-    held = exchange(share, "row", nrow, False, 1)
-    held = exchange(held, "chip", nchip, False, 2)
-    held = exchange(held, "core", 2, False, 3)
-    lfull = held.transpose(3, 2, 1, 0, 4, 5).reshape(NSUP, total, W)
+    lfull = gather(share, nrow, nchip, 1).reshape(NSUP, total, W)
 
     rows = tile_lists - row_pos * tile_rows
     rows = jnp.where((rows >= 0) & (rows < tile_rows), rows, -1)
     cols = tile_lists - col_pos * tile_cols
     cols = jnp.where((cols >= 0) & (cols < tile_cols), cols, -1)
+    rows = jnp.where(jnp.max(cols, axis=1, keepdims=True) >= 0, rows, -1)
     partial, terms = products(rows, cols, ancestor_inv, lfull)
 
-    partial = partial.reshape(NSUP, nrow, nchip, 2, count, W)
-    terms = terms.reshape(NSUP, nrow, nchip, 2, part, W)
-    sums = jnp.concatenate([partial, terms], axis=4).transpose(3, 2, 1, 0, 4, 5)
-    sums = exchange(sums, "core", 2, True, 4).sum(0)
-    sums = exchange(sums, "chip", nchip, True, 5).sum(0)
-    sums = exchange(sums, "row", nrow, True, 6).sum(0)
-    mine = sums[:, :count]
-
-    diag = exchange(sums[:, count:], "row", nrow, False, 7)
-    diag = exchange(diag, "chip", nchip, False, 8)
-    diag = exchange(diag, "core", 2, False, 9)
-    diag = diag.transpose(3, 2, 1, 0, 4, 5).reshape(NSUP, W, W)
+    sums = [
+        partial.reshape(NSUP, nrow, nchip, 2, count, W),
+        terms.reshape(NSUP, nrow, nchip, 2, part, W),
+    ]
+    sums = scatter(sums, "core", 2, 3, 2)
+    sums = scatter(sums, "chip", nchip, 2, 3)
+    mine, term = scatter(sums, "row", nrow, 1, 4)
+    diag = gather(term, nrow, nchip, 5).reshape(NSUP, W, W)
     return mine, diag_inv - diag
 
 

time: 471 us -> 197 us (0.42)
  Pallas kernels: 443 us -> 168 us
    pallas_call x9 -> x5, Pallas kernels: 428 us -> 153 us  [the longest x3 86.7 us: scatter(): pl.pallas_call(functools.partial(scatter_kernel, stage, size, axis), out_...]
    add x0 -> x6, other arithmetic: none -> 15.8 us  [scatter(): own += parts[step]]
    reduce_sum x3 -> x0, other arithmetic: 11.9 us -> none  [the longest x1 6.81 us: per_device(): sums = exchange(sums, 'core', 2, True, 4).sum(0)]
    transpose x2 -> x0, local copies, waits for them, and re-layouts: 8.63 us -> none  [the longest x1 6.75 us: per_device(): lfull = held.transpose(3, 2, 1, 0, 4, 5).reshape(NSUP, total, W)]
where the time goes in v3:
time: 197 us
  Pallas kernels  168 us (85%)
  other arithmetic  21.4 us (11%)
  local copies, waits for them, and re-layouts  7.25 us (4%)
    pallas_call x3, Pallas kernels, scatter(): pl.pallas_call(functools.partial(scatter_kernel, stage, size, axis), out_...  86.7 us
    pallas_call x2, Pallas kernels, gather(): pl.pallas_call(functools.partial(gather_kernel, nrow, nchip), out_shape=j...  66.4 us
    add x6, other arithmetic, scatter(): own += parts[step]  15.8 us
    pallas_call x1, Pallas kernels, products(): pl.pallas_call(product_kernel, out_shape=(jax.ShapeDtypeStruct((NSUP, tot...  14.4 us
    unnamed x14, local copies, waits for them, and re-layouts  4 us

profile of v3, /device:TPU:0, one launch (start us, length us, event | category | flops | bytes accessed | tf_op | source)
XLA Modules:
  0.0 196.9 jit_solution(3803671793023780372)
XLA Ops:
  0.7 0.8 fusion.1
  1.5 0.8 fusion.rows_ref
  2.2 1.6 constant_dynamic-slice_fusion.x_ref
  3.8 43.4 %shard_map.59 = f32[2,4,4,2,48,512]{5,4,3,2,1,0:T(8,128)} custom-call(f32[2,48,512]{2,1,0:T(8,128)} %constant_dynamic-slice_fusion.x_ref), custom_call_target="tpu_custom_call" | custom-call | tf_op jit(solution)/shard_map/pallas_call | solution.py:151
  47.2 1.6 bitcast_dynamic-update-slice_fusion
  48.9 14.4 %shard_map.60 = (f32[2,1536,512]{2,1,0:T(8,128)S(1)}, f32[2,512,512]{2,1,0:T(8,128)S(1)}) custom-call(s32[2,6]{1,0:T(2,128)S(1)} %fusion.rows_ref, s32[2,6]{1,0:T(2,128)S(1)} %get-tuple-element.19.cols_ref, f32[4096,2048]{1,0:T(8,128)} %a_ref.1, f32[2,1536,512]{2,1,0:T(8,128)} %bitcast.83), custom_call_target="tpu_custom_call" | custom-call | tf_op jit(solution)/shard_map/pallas_call | solution.py:206
  63.3 0.0 copy-start
  63.3 2.7 %copy-done = f32[2,1536,512]{2,1,0:T(8,128)} copy-done((f32[2,1536,512]{2,1,0:T(8,128)}, f32[2,1536,512]{2,1,0:T(8,128)S(1)}, u32[]{:S(2)}) %copy-start) | copy-done | bytes 6291480
  65.9 0.0 copy-start.1
  65.9 1.3 copy-done.1
  67.3 0.0 copy-start.2
  67.3 7.5 %shard_map.61 = (f32[1,2,4,4,48,512]{5,4,3,2,1,0:T(8,128)}, f32[1,2,4,4,16,512]{5,4,3,2,1,0:T(8,128)}) custom-call(f32[2,4,4,2,48,512]{5,4,3,2,1,0:T(8,128)} %bitcast.79, f32[2,4,4,2,16,512]{5,4,3,2,1,0:T(8,128)} %bitcast.81), custom_call_target="tpu_custom_call" | custom-call | tf_op jit(solution)/shard_map/pallas_call | solution.py:66
  74.8 0.0 copy-start.3
  74.8 0.0 copy-done.2
  74.8 2.6 %bitcast_add_fusion.1.y_ref = f32[2,4,4,16,512]{4,3,2,1,0:T(8,128)} fusion(f32[1,2,4,4,16,512]{5,4,3,2,1,0:T(8,128)} %get-tuple-element.13, f32[2,4,4,2,16,512]{5,4,3,2,1,0:T(8,128)S(1)} %bitcast.82, s32[]{:T(128)S(6)} %select_n.52), kind=kLoop, calls=%fused_computation.2 | loop fusion | flops 262144 | bytes 3145732 | tf_op jit(solution)/shard_map/add | solution.py:84
  77.4 0.0 copy-done.3
  77.4 4.6 %bitcast_add_fusion.x_ref = f32[2,4,4,48,512]{4,3,2,1,0:T(8,128)} fusion(f32[1,2,4,4,48,512]{5,4,3,2,1,0:T(8,128)S(1)} %copy-done.3, f32[2,4,4,2,48,512]{5,4,3,2,1,0:T(8,128)} %bitcast.80, s32[]{:T(128)S(6)} %select_n.52), kind=kLoop, calls=%fused_computation | loop fusion | flops 786432 | bytes 9437188 | tf_op jit(solution)/shard_map/add | solution.py:84
  82.0 50.9 %shard_map.62 = (f32[3,2,4,48,512]{4,3,2,1,0:T(8,128)}, f32[3,2,4,16,512]{4,3,2,1,0:T(8,128)}) custom-call(f32[2,4,4,48,512]{4,3,2,1,0:T(8,128)} %bitcast_add_fusion.x_ref, f32[2,4,4,16,512]{4,3,2,1,0:T(8,128)} %bitcast_add_fusion.1.y_ref), custom_call_target="tpu_custom_call" | custom-call | tf_op jit(solution)/shard_map/pallas_call | solution.py:66
  132.8 2.0 %bitcast_add_fusion.5.y_ref = f32[2,4,16,512]{3,2,1,0:T(8,128)} fusion(f32[3,2,4,16,512]{4,3,2,1,0:T(8,128)} %get-tuple-element.15, f32[2,4,4,16,512]{4,3,2,1,0:T(8,128)} %bitcast_add_fusion.1.y_ref, s32[]{:T(128)S(6)} %select_n.51), kind=kLoop, calls=%fused_computation.6 | loop fusion | flops 196608 | bytes 1310724 | tf_op jit(solution)/shard_map/add | solution.py:84
  134.8 0.0 copy-start.5
  134.8 3.1 %bitcast_add_fusion.2.x_ref = f32[2,4,48,512]{3,2,1,0:T(8,128)} fusion(f32[3,2,4,48,512]{4,3,2,1,0:T(8,128)} %get-tuple-element.14, f32[2,4,4,48,512]{4,3,2,1,0:T(8,128)} %bitcast_add_fusion.x_ref, s32[]{:T(128)S(6)} %select_n.51), kind=kLoop, calls=%fused_computation.3 | loop fusion | flops 589824 | bytes 3932164 | tf_op jit(solution)/shard_map/add | solution.py:84
  137.9 0.0 copy-start.4
  137.9 28.3 %shard_map.63 = (f32[3,2,48,512]{3,2,1,0:T(8,128)}, f32[3,2,16,512]{3,2,1,0:T(8,128)}) custom-call(f32[2,4,48,512]{3,2,1,0:T(8,128)} %bitcast_add_fusion.2.x_ref, f32[2,4,16,512]{3,2,1,0:T(8,128)} %bitcast_add_fusion.5.y_ref), custom_call_target="tpu_custom_call" | custom-call | tf_op jit(solution)/shard_map/pallas_call | solution.py:66
  166.3 0.0 copy-start.6
  166.3 2.0 %bitcast_add_fusion.8 = f32[2,48,512]{2,1,0:T(8,128)} fusion(f32[3,2,48,512]{3,2,1,0:T(8,128)} %get-tuple-element.16, f32[2,4,48,512]{3,2,1,0:T(8,128)} %bitcast_add_fusion.2.x_ref, s32[]{:T(128)S(6)} %select_n.49), kind=kLoop, calls=%fused_computation.9 | loop fusion | flops 147456 | bytes 983044 | tf_op jit(solution)/shard_map/add | solution.py:84
  168.3 0.0 copy-done.5
  168.3 1.6 bitcast_add_fusion.14.x_ref
  169.8 23.0 %shard_map.64 = f32[2,4,4,2,16,512]{5,4,3,2,1,0:T(8,128)} custom-call(f32[2,16,512]{2,1,0:T(8,128)} %bitcast_add_fusion.14.x_ref), custom_call_target="tpu_custom_call" | custom-call | tf_op jit(solution)/shard_map/pallas_call | solution.py:151
  192.8 0.0 copy-done.6
  192.9 0.7 bitcast_dynamic-update-slice_fusion.1
  193.5 0.0 copy-done.4
  193.5 3.4 %bitcast_subtract_fusion = f32[2,512,512]{2,1,0:T(8,128)} fusion(f32[2,512,512]{2,1,0:T(8,128)S(1)} %copy-done.4, f32[2,4,4,2,16,512]{5,4,3,2,1,0:T(8,128)} %bitcast_dynamic-update-slice_fusion.1), kind=kLoop, calls=%fused_computation.1 | loop fusion | flops 524288 | bytes 6291456 | tf_op jit(solution)/shard_map/sub | solution.py:256
  (1 shorter events, 0.0 us)
Async XLA Ops:
  63.3 2.7 %copy-start = (f32[2,1536,512]{2,1,0:T(8,128)}, f32[2,1536,512]{2,1,0:T(8,128)S(1)}, u32[]{:S(2)}) copy-start(f32[2,1536,512]{2,1,0:T(8,128)S(1)} %get-tuple-element.10) | copy-start | bytes 18874372
  65.9 1.3 copy-start.1
  67.3 7.6 %copy-start.2 = (f32[2,512,512]{2,1,0:T(8,128)S(1)}, f32[2,512,512]{2,1,0:T(8,128)}, u32[]{:S(2)}) copy-start(f32[2,512,512]{2,1,0:T(8,128)} %copy-done.1) | copy-start | bytes 6291460
  74.8 2.6 %copy-start.3 = (f32[1,2,4,4,48,512]{5,4,3,2,1,0:T(8,128)S(1)}, f32[1,2,4,4,48,512]{5,4,3,2,1,0:T(8,128)}, u32[]{:S(2)}) copy-start(f32[1,2,4,4,48,512]{5,4,3,2,1,0:T(8,128)} %get-tuple-element.12) | copy-start | bytes 9437188
  134.8 33.5 %copy-start.5 = (f32[2,4,16,512]{3,2,1,0:T(8,128)S(1)}, f32[2,4,16,512]{3,2,1,0:T(8,128)}, u32[]{:S(2)}) copy-start(f32[2,4,16,512]{3,2,1,0:T(8,128)} %bitcast_add_fusion.5.y_ref) | copy-start | bytes 786436
  137.9 55.6 %copy-start.4 = (f32[2,512,512]{2,1,0:T(8,128)S(1)}, f32[2,512,512]{2,1,0:T(8,128)}, u32[]{:S(2)}) copy-start(f32[2,512,512]{2,1,0:T(8,128)} %param.6) | copy-start | bytes 6291460
  166.3 26.6 %copy-start.6 = (f32[3,2,16,512]{3,2,1,0:T(8,128)S(1)}, f32[3,2,16,512]{3,2,1,0:T(8,128)}, u32[]{:S(2)}) copy-start(f32[3,2,16,512]{3,2,1,0:T(8,128)} %get-tuple-element.17) | copy-start | bytes 589828

commit v4 on v3

--- a/solution.py
+++ b/solution.py
@@ -38,52 +38,131 @@
     return [device(lax.rem(me + step, size)) for step in range(1, size)]
 
 
-def scatter_kernel(stage, size, axis, x_ref, y_ref, x_out, y_out, send_sem, recv_sem):
-    me, _ = place(stage)
-    peers = others(stage, size)
-    enter(peers)
-    copies = []
-    lead = (slice(None),) * axis
-    for step, peer in enumerate(peers):
-        to = lax.rem(me + step + 1, size)
-        for which, (src, dst) in enumerate(((x_ref, x_out), (y_ref, y_out))):
-            copy = pltpu.make_async_remote_copy(
-                src_ref=src.at[lead + (to,)],
-                dst_ref=dst.at[step],
-                send_sem=send_sem.at[step, which],
-                recv_sem=recv_sem.at[step, which],
-                device_id=peer,
-                device_id_type=MESH,
+def send(src, dst, send_sem, recv_sem, peer):
+    copy = pltpu.make_async_remote_copy(
+        src_ref=src,
+        dst_ref=dst,
+        send_sem=send_sem,
+        recv_sem=recv_sem,
+        device_id=peer,
+        device_id_type=MESH,
+    )
+    copy.start()
+    return copy
+
+
+def scatter_kernel(
+    nrow, nchip, x_ref, y_ref, x_out, y_out, core_x, core_y, held, chip_in, sums, row_in, *sems
+):
+    core_send, core_recv, chip_send, chip_recv, row_send, row_recv = sems
+    row, _ = place("row")
+    chip, _ = place("chip")
+    core, _ = place("core")
+    rows, chips, cores = others("row", nrow), others("chip", nchip), others("core", 2)
+    enter(rows + chips + cores)
+    count = x_ref.shape[-2]
+    pieces = [(step, sup) for step in [*range(1, nrow), 0] for sup in range(NSUP)]
+    owners = [lax.rem(row + step, nrow) for step, _ in pieces]
+    from_core = []
+    for at, (_, sup) in enumerate(pieces):
+        to = owners[at]
+        from_core.append(
+            [
+                send(
+                    src.at[sup, to, :, 1 - core],
+                    dst.at[at],
+                    core_send.at[at, which],
+                    core_recv.at[at, which],
+                    cores[0],
+                )
+                for which, (src, dst) in enumerate(((x_ref, core_x), (y_ref, core_y)))
+            ]
+        )
+    from_chips = []
+    from_rows = []
+
+    def finish(at):
+        step, sup = pieces[at]
+        for copy in from_chips[at]:
+            copy.wait_recv()
+        total = held[at, chip]
+        for near in range(nchip - 1):
+            total += chip_in[at, near]
+        sums[at] = total
+        if step > 0:
+            from_rows.append(
+                send(
+                    sums.at[at],
+                    row_in.at[at],
+                    row_send.at[at],
+                    row_recv.at[at],
+                    rows[step - 1],
+                )
             )
-            copy.start()
-            copies.append(copy)
-    for copy in copies:
-        copy.wait()
-
-
-def scatter(pair, stage, size, axis, collective_id):
-    shapes = [(size - 1,) + x.shape[:axis] + x.shape[axis + 1:] for x in pair]
-    moved = pl.pallas_call(
-        functools.partial(scatter_kernel, stage, size, axis),
-        out_shape=[jax.ShapeDtypeStruct(shape, jnp.float32) for shape in shapes],
-        in_specs=[pl.BlockSpec(memory_space=pl.ANY)] * 2,
-        out_specs=[pl.BlockSpec(memory_space=pl.ANY)] * 2,
+
+    for at, (_, sup) in enumerate(pieces):
+        for copy in from_core[at]:
+            copy.wait_recv()
+        held[at, :, :count] = x_ref[sup, owners[at], :, core] + core_x[at]
+        held[at, :, count:] = y_ref[sup, owners[at], :, core] + core_y[at]
+        from_chips.append(
+            [
+                send(
+                    held.at[at, lax.rem(chip + near + 1, nchip)],
+                    chip_in.at[at, near],
+                    chip_send.at[at, near],
+                    chip_recv.at[at, near],
+                    peer,
+                )
+                for near, peer in enumerate(chips)
+            ]
+        )
+        if at >= 2:
+            finish(at - 2)
+    finish(len(pieces) - 2)
+    finish(len(pieces) - 1)
+    for copy in from_rows:
+        copy.wait_recv()
+    for sup in range(NSUP):
+        total = sums[(nrow - 1) * NSUP + sup]
+        for step in range(nrow - 1):
+            total += row_in[step * NSUP + sup]
+        x_out[sup] = total[:count]
+        y_out[sup] = total[count:]
+    for group in from_core + from_chips + [from_rows]:
+        for copy in group:
+            copy.wait_send()
+
+
+def scatter(x, y, nrow, nchip, collective_id):
+    count, part = x.shape[-2], y.shape[-2]
+    n = nrow * NSUP
+    f32 = jnp.float32
+    vmem = pl.BlockSpec(memory_space=pltpu.VMEM)
+    core, chip, row = (n, 2), (n, nchip - 1), (n - NSUP,)
+    return pl.pallas_call(
+        functools.partial(scatter_kernel, nrow, nchip),
+        out_shape=[
+            jax.ShapeDtypeStruct((NSUP, count, W), f32),
+            jax.ShapeDtypeStruct((NSUP, part, W), f32),
+        ],
+        in_specs=[vmem, vmem],
+        out_specs=[vmem, vmem],
         scratch_shapes=[
-            pltpu.SemaphoreType.DMA((size - 1, 2)),
-            pltpu.SemaphoreType.DMA((size - 1, 2)),
+            pltpu.VMEM((n, nchip, count, W), f32),
+            pltpu.VMEM((n, nchip, part, W), f32),
+            pltpu.VMEM((n, nchip, count + part, W), f32),
+            pltpu.VMEM((n, nchip - 1, count + part, W), f32),
+            pltpu.VMEM((n, count + part, W), f32),
+            pltpu.VMEM((n - NSUP, count + part, W), f32),
+            *(pltpu.SemaphoreType.DMA(s) for s in (core, core, chip, chip, row, row)),
         ],
         compiler_params=pltpu.CompilerParams(
-            collective_id=collective_id, has_side_effects=True
+            collective_id=collective_id,
+            has_side_effects=True,
+            vmem_limit_bytes=44 * 1024 * 1024,
         ),
-    )(*pair)
-    me, _ = place(stage)
-    sums = []
-    for x, parts in zip(pair, moved):
-        own = lax.dynamic_index_in_dim(x, me, axis, keepdims=False)
-        for step in range(size - 1):
-            own += parts[step]
-        sums.append(own)
-    return sums
+    )(x, y)
 
 
 def gather_kernel(nrow, nchip, x_ref, out_ref, *sems):
@@ -95,22 +174,13 @@
     enter(rows + chips + cores)
     started = []
 
-    def send(src, slot, send_sem, recv_sem, peer):
-        copy = pltpu.make_async_remote_copy(
-            src_ref=src,
-            dst_ref=slot,
-            send_sem=send_sem,
-            recv_sem=recv_sem,
-            device_id=peer,
-            device_id_type=MESH,
-        )
-        copy.start()
-        started.append(copy)
-        return copy
+    def forward(*args):
+        started.append(send(*args))
+        return started[-1]
 
     mine = out_ref.at[:, row, chip, core]
     from_rows = [
-        send(x_ref, mine, row_send.at[step], row_recv.at[step], peer)
+        forward(x_ref, mine, row_send.at[step], row_recv.at[step], peer)
         for step, peer in enumerate(rows)
     ]
     from_chips = []
@@ -127,17 +197,17 @@
                 (
                     near,
                     step + 1,
-                    send(src, slot, chip_send.at[step, near], chip_recv.at[step, near], peer),
+                    forward(src, slot, chip_send.at[step, near], chip_recv.at[step, near], peer),
                 )
             )
-        last.append(send(src, slot, core_send.at[0, near], core_recv.at[0, near], cores[0]))
+        last.append(forward(src, slot, core_send.at[0, near], core_recv.at[0, near], cores[0]))
     for near, step, copy in from_chips:
         copy.wait_recv()
         slot = out_ref.at[
             :, lax.rem(row - near + nrow, nrow), lax.rem(chip - step + nchip, nchip), core
         ]
         last.append(
-            send(slot, slot, core_send.at[step, near], core_recv.at[step, near], cores[0])
+            forward(slot, slot, core_send.at[step, near], core_recv.at[step, near], cores[0])
         )
     for copy in last:
         copy.wait_recv()
@@ -245,13 +315,13 @@
     rows = jnp.where(jnp.max(cols, axis=1, keepdims=True) >= 0, rows, -1)
     partial, terms = products(rows, cols, ancestor_inv, lfull)
 
-    sums = [
+    mine, term = scatter(
         partial.reshape(NSUP, nrow, nchip, 2, count, W),
         terms.reshape(NSUP, nrow, nchip, 2, part, W),
-    ]
-    sums = scatter(sums, "core", 2, 3, 2)
-    sums = scatter(sums, "chip", nchip, 2, 3)
-    mine, term = scatter(sums, "row", nrow, 1, 4)
+        nrow,
+        nchip,
+        2,
+    )
     diag = gather(term, nrow, nchip, 5).reshape(NSUP, W, W)
     return mine, diag_inv - diag
 

time: 197 us -> 148 us (0.75)
  Pallas kernels: 168 us -> 138 us
  other arithmetic: 21.4 us -> 4.95 us
  local copies, waits for them, and re-layouts: 7.25 us -> 5.2 us
    pallas_call x3 -> x1, Pallas kernels: 86.7 us -> 59.8 us  [scatter(): pl.pallas_call(functools.partial(scatter_kernel, nrow, nchip), out_shape=...]
    add x6 -> x0, other arithmetic: 15.8 us -> none  [scatter(): own += parts[step]]
    pallas_call x2, Pallas kernels: 66.4 us -> 63.3 us  [gather(): pl.pallas_call(functools.partial(gather_kernel, nrow, nchip), out_shape=j...]
    unnamed x14 -> x7, local copies, waits for them, and re-layouts: 4 us -> 1.31 us
where the time goes in v4:
time: 148 us; the launch traced here: 149 us
  Pallas kernels  138 us (93%)
  local copies, waits for them, and re-layouts  5.2 us (4%)
  other arithmetic  4.95 us (3%)
    pallas_call x2, Pallas kernels, gather(): pl.pallas_call(functools.partial(gather_kernel, nrow, nchip), out_shape=j...  63.3 us
    pallas_call x1, Pallas kernels, scatter(): pl.pallas_call(functools.partial(scatter_kernel, nrow, nchip), out_shape=...  59.8 us
    pallas_call x1, Pallas kernels, products(): pl.pallas_call(product_kernel, out_shape=(jax.ShapeDtypeStruct((NSUP, tot...  15.2 us
    sub x1, other arithmetic, per_device(): return (mine, diag_inv - diag)  3.39 us

profile of v4, /device:TPU:0, one launch (start us, length us, event | category | flops | bytes accessed | tf_op | source)
XLA Modules:
  0.0 149.2 jit_solution(14499292032142523779)
XLA Ops:
  0.7 0.8 fusion.1
  1.5 0.8 fusion.rows_ref
  2.2 1.6 %constant_dynamic-slice_fusion.x_ref = f32[2,48,512]{2,1,0:T(8,128)} fusion(f32[2,384,512]{2,1,0:T(8,128)} %param.5, s32[]{:T(128)S(6)} %select_n.35), kind=kLoop, calls=%fused_computation.6 | loop fusion | bytes 393220 | tf_op jit(solution)/shard_map/dynamic_slice | solution.py:308
  3.8 43.4 %shard_map.59 = f32[2,4,4,2,48,512]{5,4,3,2,1,0:T(8,128)} custom-call(f32[2,48,512]{2,1,0:T(8,128)} %constant_dynamic-slice_fusion.x_ref), custom_call_target="tpu_custom_call" | custom-call | tf_op jit(solution)/shard_map/pallas_call | solution.py:221
  47.2 1.6 %bitcast_dynamic-update-slice_fusion = f32[2,4,4,2,48,512]{5,4,3,2,1,0:T(8,128)} fusion(f32[2,4,4,2,48,512]{5,4,3,2,1,0:T(8,128)} %shard_map.59, s32[]{:T(128)S(6)} %select_n.36, s32[]{:T(128)S(6)} %select_n.38, s32[]{:T(128)S(6)} %select_n.39, f32[2,384,512]{2,1,0:T(8,128)} %param.5, s32[]{:T(128)S(6)} %select_n.35), kind=kLoop, calls=%fused_computation.1 | loop fusion | bytes 393232 | tf_op jit(solution)/shard_map/dynamic_update_slice | solution.py:234
  48.9 15.2 %shard_map.60 = (f32[2,1536,512]{2,1,0:T(8,128)S(1)}, f32[2,512,512]{2,1,0:T(8,128)S(1)}) custom-call(s32[2,6]{1,0:T(2,128)S(1)} %fusion.rows_ref, s32[2,6]{1,0:T(2,128)S(1)} %get-tuple-element.11.cols_ref, f32[4096,2048]{1,0:T(8,128)} %a_ref.1, f32[2,1536,512]{2,1,0:T(8,128)} %bitcast.11), custom_call_target="tpu_custom_call" | custom-call | tf_op jit(solution)/shard_map/pallas_call | solution.py:276
  64.1 59.8 %shard_map.61 = (f32[2,48,512]{2,1,0:T(8,128)S(1)}, f32[2,16,512]{2,1,0:T(8,128)S(1)}) custom-call(f32[2,4,4,2,48,512]{5,4,3,2,1,0:T(8,128)S(1)} %bitcast.9, f32[2,4,4,2,16,512]{5,4,3,2,1,0:T(8,128)S(1)} %bitcast.10), custom_call_target="tpu_custom_call" | custom-call | tf_op jit(solution)/shard_map/pallas_call | solution.py:143
  123.9 0.0 copy-start
  123.9 0.6 copy-done
  124.5 0.0 copy-start.2
  124.5 0.0 copy-start.1
  124.5 20.0 %shard_map.62 = f32[2,4,4,2,16,512]{5,4,3,2,1,0:T(8,128)} custom-call(f32[2,16,512]{2,1,0:T(8,128)} %copy-done), custom_call_target="tpu_custom_call" | custom-call | tf_op jit(solution)/shard_map/pallas_call | solution.py:221
  144.5 0.0 copy-done.1
  144.5 0.6 bitcast_dynamic-update-slice_fusion.1
  145.1 0.0 copy-done.2
  145.1 3.4 %bitcast_subtract_fusion = f32[2,512,512]{2,1,0:T(8,128)} fusion(f32[2,512,512]{2,1,0:T(8,128)S(1)} %copy-done.2, f32[2,4,4,2,16,512]{5,4,3,2,1,0:T(8,128)} %bitcast_dynamic-update-slice_fusion.1), kind=kLoop, calls=%fused_computation | loop fusion | flops 524288 | bytes 6291456 | tf_op jit(solution)/shard_map/sub | solution.py:326
  148.5 0.7 copy.9
  (1 shorter events, 0.0 us)
Async XLA Ops:
  123.9 0.6 copy-start
  124.5 20.6 %copy-start.2 = (f32[2,512,512]{2,1,0:T(8,128)S(1)}, f32[2,512,512]{2,1,0:T(8,128)}, u32[]{:S(2)}) copy-start(f32[2,512,512]{2,1,0:T(8,128)} %param.6) | copy-start | bytes 6291460
  124.5 20.0 %copy-start.1 = (f32[2,16,512]{2,1,0:T(8,128)S(1)}, f32[2,16,512]{2,1,0:T(8,128)}, u32[]{:S(2)}) copy-start(f32[2,16,512]{2,1,0:T(8,128)} %copy-done) | copy-start | bytes 196612

commit v5 on v4

--- a/solution.py
+++ b/solution.py
@@ -234,43 +234,52 @@
     return lax.dynamic_update_slice(full, x[:, None, None, None], where)
 
 
-def product_kernel(rows_ref, cols_ref, a_ref, l_ref, p_ref, d_ref):
-    sup, i, j = pl.program_id(0), pl.program_id(1), pl.program_id(2)
-    highest = lax.Precision.HIGHEST
+def dot(a, b, contract):
+    def split(x):
+        high = x.astype(jnp.bfloat16)
+        return high, (x - high.astype(jnp.float32)).astype(jnp.bfloat16)
+
+    def one(x, y):
+        return lax.dot_general(
+            x, y, ((contract, (0,)), ((), ())), preferred_element_type=jnp.float32
+        )
+
+    a_high, a_low = split(a)
+    b_high, b_low = split(b)
+    return one(a_low, b_high) + one(a_high, b_low) + one(a_high, b_high)
+
+
+def product_kernel(rows_ref, cols_ref, *refs):
+    *tiles, l_ref, p_ref, d_ref = refs
+    sup, i = pl.program_id(0), pl.program_id(1)
     row_hit = rows_ref[sup, i] >= 0
 
-    @pl.when((i == 0) & (j == 0))
+    @pl.when(i == 0)
     def _():
         d_ref[...] = jnp.zeros_like(d_ref)
 
-    @pl.when(j == 0)
+    p_ref[...] = jnp.zeros_like(p_ref)
+
+    @pl.when(row_hit)
     def _():
-        p_ref[...] = jnp.zeros_like(p_ref)
-
-    @pl.when(row_hit & (cols_ref[sup, j] >= 0))
-    def _():
-        block = l_ref[0, pl.ds(pl.multiple_of(j * TILE, TILE), TILE), :]
-        p_ref[0] -= jnp.dot(
-            a_ref[...], block, precision=highest, preferred_element_type=jnp.float32
-        )
-
-    @pl.when(row_hit & (j == NS - 1))
-    def _():
+        for j, a_ref in enumerate(tiles):
+
+            @pl.when(cols_ref[sup, j] >= 0)
+            def _():
+                p_ref[0] -= dot(a_ref[...], l_ref[0, j * TILE:(j + 1) * TILE, :], (1,))
+
         block = l_ref[0, pl.ds(pl.multiple_of(i * TILE, TILE), TILE), :]
-        d_ref[0] += lax.dot_general(
-            block,
-            p_ref[0],
-            (((0,), (0,)), ((), ())),
-            precision=highest,
-            preferred_element_type=jnp.float32,
-        )
+        d_ref[0] += dot(block, p_ref[0], (0,))
 
 
 def products(rows, cols, ancestor, lfull):
-    def a_map(sup, i, j, rows_ref, cols_ref):
-        row, col = rows_ref[sup, i], cols_ref[sup, j]
-        hit = (row >= 0) & (col >= 0)
-        return jnp.where(hit, row, 0), jnp.where(hit, col, 0)
+    def tile(j):
+        def index(sup, i, rows_ref, cols_ref):
+            row, col = rows_ref[sup, i], cols_ref[sup, j]
+            hit = (row >= 0) & (col >= 0)
+            return jnp.where(hit, row, 0), jnp.where(hit, col, 0)
+
+        return pl.BlockSpec((TILE, TILE), index)
 
     total = lfull.shape[1]
     return pl.pallas_call(
@@ -281,18 +290,16 @@
         ),
         grid_spec=pltpu.PrefetchScalarGridSpec(
             num_scalar_prefetch=2,
-            grid=(NSUP, NS, NS),
-            in_specs=[
-                pl.BlockSpec((TILE, TILE), a_map),
-                pl.BlockSpec((1, total, W), lambda sup, i, j, *_: (sup, 0, 0)),
-            ],
+            grid=(NSUP, NS),
+            in_specs=[tile(j) for j in range(NS)]
+            + [pl.BlockSpec((1, total, W), lambda sup, i, *_: (sup, 0, 0))],
             out_specs=[
-                pl.BlockSpec((1, TILE, W), lambda sup, i, j, *_: (sup, i, 0)),
-                pl.BlockSpec((1, W, W), lambda sup, i, j, *_: (sup, 0, 0)),
+                pl.BlockSpec((1, TILE, W), lambda sup, i, *_: (sup, i, 0)),
+                pl.BlockSpec((1, W, W), lambda sup, i, *_: (sup, 0, 0)),
             ],
         ),
         compiler_params=pltpu.CompilerParams(vmem_limit_bytes=40 * 1024 * 1024),
-    )(rows, cols, ancestor, lfull)
+    )(rows, cols, *[ancestor] * NS, lfull)
 
 
 def per_device(nrow, ncol, ancestor_inv, l_scaled, diag_inv, tile_lists):

time: 148 us -> 140 us (0.946); the launches traced: 149 us -> 140 us
  Pallas kernels: 138 us -> 129 us
    pallas_call x1, Pallas kernels: 59.8 us -> 51.6 us  [scatter(): pl.pallas_call(functools.partial(scatter_kernel, nrow, nchip), out_shape=...]
where the time goes in v5:
time: 140 us
  Pallas kernels  129 us (92%)
  local copies, waits for them, and re-layouts  5.2 us (4%)
  other arithmetic  4.95 us (4%)
    pallas_call x2, Pallas kernels, gather(): pl.pallas_call(functools.partial(gather_kernel, nrow, nchip), out_shape=j...  62.6 us
    pallas_call x1, Pallas kernels, scatter(): pl.pallas_call(functools.partial(scatter_kernel, nrow, nchip), out_shape=...  51.6 us
    pallas_call x1, Pallas kernels, products(): pl.pallas_call(product_kernel, out_shape=(jax.ShapeDtypeStruct((NSUP, tot...  14.5 us
    sub x1, other arithmetic, per_device(): return (mine, diag_inv - diag)  3.39 us

profile of v5, /device:TPU:0, one launch (start us, length us, event | category | flops | bytes accessed | tf_op | source)
XLA Modules:
  0.0 139.6 jit_solution(10672340044344452787)
XLA Ops:
  0.7 0.8 fusion.1
  1.5 0.8 fusion.rows_ref
  2.2 1.6 %constant_dynamic-slice_fusion.x_ref = f32[2,48,512]{2,1,0:T(8,128)} fusion(f32[2,384,512]{2,1,0:T(8,128)} %param.5, s32[]{:T(128)S(6)} %select_n.35), kind=kLoop, calls=%fused_computation.6 | loop fusion | bytes 393220 | tf_op jit(solution)/shard_map/dynamic_slice | solution.py:315
  3.8 43.4 %shard_map.59 = f32[2,4,4,2,48,512]{5,4,3,2,1,0:T(8,128)} custom-call(f32[2,48,512]{2,1,0:T(8,128)} %constant_dynamic-slice_fusion.x_ref), custom_call_target="tpu_custom_call" | custom-call | tf_op jit(solution)/shard_map/pallas_call | solution.py:221
  47.2 1.6 %bitcast_dynamic-update-slice_fusion = f32[2,4,4,2,48,512]{5,4,3,2,1,0:T(8,128)} fusion(f32[2,4,4,2,48,512]{5,4,3,2,1,0:T(8,128)} %shard_map.59, s32[]{:T(128)S(6)} %select_n.36, s32[]{:T(128)S(6)} %select_n.38, s32[]{:T(128)S(6)} %select_n.39, f32[2,384,512]{2,1,0:T(8,128)} %param.5, s32[]{:T(128)S(6)} %select_n.35), kind=kLoop, calls=%fused_computation.1 | loop fusion | bytes 393232 | tf_op jit(solution)/shard_map/dynamic_update_slice | solution.py:234
  48.9 14.5 %shard_map.60 = (f32[2,1536,512]{2,1,0:T(8,128)S(1)}, f32[2,512,512]{2,1,0:T(8,128)S(1)}) custom-call(s32[2,6]{1,0:T(2,128)S(1)} %fusion.rows_ref, s32[2,6]{1,0:T(2,128)S(1)} %get-tuple-element.11.cols_ref, f32[4096,2048]{1,0:T(8,128)} %refs_5_.1, f32[4096,2048]{1,0:T(8,128)} %refs_5_.1, f32[4096,2048]{1,0:T(8,128)} %refs_5_.1, f32[4096,2048]{1,0:T(8,128)} %refs_5_.1, ...), custom_call_target="tpu_custom_call" | custom-call | tf_op jit(solution)/shard_map/pallas_call | solution.py:285
  63.3 51.6 %shard_map.61 = (f32[2,48,512]{2,1,0:T(8,128)S(1)}, f32[2,16,512]{2,1,0:T(8,128)S(1)}) custom-call(f32[2,4,4,2,48,512]{5,4,3,2,1,0:T(8,128)S(1)} %bitcast.9, f32[2,4,4,2,16,512]{5,4,3,2,1,0:T(8,128)S(1)} %bitcast.10), custom_call_target="tpu_custom_call" | custom-call | tf_op jit(solution)/shard_map/pallas_call | solution.py:143
  114.9 0.0 copy-start
  114.9 0.6 copy-done
  115.6 0.0 copy-start.2
  115.6 0.0 copy-start.1
  115.6 19.3 %shard_map.62 = f32[2,4,4,2,16,512]{5,4,3,2,1,0:T(8,128)} custom-call(f32[2,16,512]{2,1,0:T(8,128)} %copy-done), custom_call_target="tpu_custom_call" | custom-call | tf_op jit(solution)/shard_map/pallas_call | solution.py:221
  134.8 0.0 copy-done.1
  134.8 0.6 bitcast_dynamic-update-slice_fusion.1
  135.5 0.0 copy-done.2
  135.5 3.4 %bitcast_subtract_fusion = f32[2,512,512]{2,1,0:T(8,128)} fusion(f32[2,512,512]{2,1,0:T(8,128)S(1)} %copy-done.2, f32[2,4,4,2,16,512]{5,4,3,2,1,0:T(8,128)} %bitcast_dynamic-update-slice_fusion.1), kind=kLoop, calls=%fused_computation | loop fusion | flops 524288 | bytes 6291456 | tf_op jit(solution)/shard_map/sub | solution.py:333
  138.9 0.7 copy.9
  (1 shorter events, 0.0 us)
Async XLA Ops:
  114.9 0.6 copy-start
  115.6 19.9 %copy-start.2 = (f32[2,512,512]{2,1,0:T(8,128)S(1)}, f32[2,512,512]{2,1,0:T(8,128)}, u32[]{:S(2)}) copy-start(f32[2,512,512]{2,1,0:T(8,128)} %param.6) | copy-start | bytes 6291460
  115.6 19.3 %copy-start.1 = (f32[2,16,512]{2,1,0:T(8,128)S(1)}, f32[2,16,512]{2,1,0:T(8,128)}, u32[]{:S(2)}) copy-start(f32[2,16,512]{2,1,0:T(8,128)} %copy-done) | copy-start | bytes 196612

commit v6 on v5

--- a/solution.py
+++ b/solution.py
@@ -165,7 +165,7 @@
     )(x, y)
 
 
-def gather_kernel(nrow, nchip, x_ref, out_ref, *sems):
+def gather_kernel(nrow, nchip, known, x_ref, out_ref, *sems):
     row_send, row_recv, chip_send, chip_recv, core_send, core_recv = sems
     row, _ = place("row")
     chip, _ = place("chip")
@@ -185,7 +185,7 @@
     ]
     from_chips = []
     last = []
-    for near in range(nrow):
+    for near in range(1 if known else 0, nrow):
         src = x_ref
         slot = mine
         if near > 0:
@@ -215,11 +215,11 @@
         copy.wait_send()
 
 
-def gather(x, nrow, nchip, collective_id):
+def gather(x, nrow, nchip, collective_id, plane=None):
     shape = (x.shape[0], nrow, nchip, 2) + x.shape[1:]
     row, chip, core = ((nrow - 1,), (nchip - 1, nrow), (nchip, nrow))
     full = pl.pallas_call(
-        functools.partial(gather_kernel, nrow, nchip),
+        functools.partial(gather_kernel, nrow, nchip, plane is not None),
         out_shape=jax.ShapeDtypeStruct(shape, x.dtype),
         in_specs=[pl.BlockSpec(memory_space=pl.ANY)],
         out_specs=pl.BlockSpec(memory_space=pl.ANY),
@@ -230,6 +230,9 @@
             collective_id=collective_id, has_side_effects=True
         ),
     )(x)
+    if plane is not None:
+        plane = plane.reshape(x.shape[0], 1, nchip, 2, *x.shape[1:])
+        return lax.dynamic_update_slice(full, plane, (0, place("row")[0], 0, 0, 0, 0))
     where = (0, place("row")[0], place("chip")[0], place("core")[0], 0, 0)
     return lax.dynamic_update_slice(full, x[:, None, None, None], where)
 
@@ -313,7 +316,7 @@
     total = l_scaled.shape[1] * nrow
 
     share = lax.dynamic_slice_in_dim(l_scaled, col_pos * count, count, 1)
-    lfull = gather(share, nrow, nchip, 1).reshape(NSUP, total, W)
+    lfull = gather(share, nrow, nchip, 1, l_scaled).reshape(NSUP, total, W)
 
     rows = tile_lists - row_pos * tile_rows
     rows = jnp.where((rows >= 0) & (rows < tile_rows), rows, -1)

time: 140 us -> 137 us (0.979); the launches traced: 140 us -> 135 us
  Pallas kernels: 129 us -> 126 us
    pallas_call x1, Pallas kernels: 14.5 us -> 12.2 us  [products(): pl.pallas_call(product_kernel, out_shape=(jax.ShapeDtypeStruct((NSUP, tot...]
    pallas_call x2, Pallas kernels: 62.6 us -> 60.8 us  [gather(): pl.pallas_call(functools.partial(gather_kernel, nrow, nchip, plane is not...]
    dynamic_update_slice x2 -> x1, local copies, waits for them, and re-layouts: 2.27 us -> 0.64 us  [gather(): return lax.dynamic_update_slice(full, x[:, None, None, None], where)]
where the time goes in v6:
time: 137 us; the launch traced here: 135 us
  Pallas kernels  126 us (92%)
  local copies, waits for them, and re-layouts  4.91 us (4%)
  other arithmetic  3.59 us (3%)
    pallas_call x2, Pallas kernels, gather(): pl.pallas_call(functools.partial(gather_kernel, nrow, nchip, plane is not...  60.8 us
    pallas_call x1, Pallas kernels, scatter(): pl.pallas_call(functools.partial(scatter_kernel, nrow, nchip), out_shape=...  52.8 us
    pallas_call x1, Pallas kernels, products(): pl.pallas_call(product_kernel, out_shape=(jax.ShapeDtypeStruct((NSUP, tot...  12.2 us
    sub x1, other arithmetic, per_device(): return (mine, diag_inv - diag)  3.39 us

profile of v6, /device:TPU:0, one launch (start us, length us, event | category | flops | bytes accessed | tf_op | source)
XLA Modules:
  0.0 135.0 jit_solution(17272789660594839541)
XLA Ops:
  0.6 1.6 %constant_dynamic-slice_fusion.x_ref = f32[2,48,512]{2,1,0:T(8,128)} fusion(f32[2,384,512]{2,1,0:T(8,128)} %param.5, s32[]{:T(128)S(6)} %select_n.32), kind=kLoop, calls=%fused_computation.6 | loop fusion | bytes 393220 | tf_op jit(solution)/shard_map/dynamic_slice | solution.py:318
  2.3 0.0 copy-start.3
  2.3 40.8 %shard_map.59 = f32[2,4,4,2,48,512]{5,4,3,2,1,0:T(8,128)} custom-call(f32[2,48,512]{2,1,0:T(8,128)} %constant_dynamic-slice_fusion.x_ref), custom_call_target="tpu_custom_call" | custom-call | tf_op jit(solution)/shard_map/pallas_call | solution.py:221
  43.1 0.0 copy-start.4
  43.1 0.0 copy-done.3
  43.1 1.3 constant_dynamic-update-slice_fusion
  44.4 0.0 copy-done.4
  44.4 0.1 fusion.1
  44.6 0.1 fusion.rows_ref
  44.6 12.2 %shard_map.60 = (f32[2,1536,512]{2,1,0:T(8,128)S(1)}, f32[2,512,512]{2,1,0:T(8,128)S(1)}) custom-call(s32[2,6]{1,0:T(2,128)S(1)} %fusion.rows_ref, s32[2,6]{1,0:T(2,128)S(1)} %get-tuple-element.11.cols_ref, f32[4096,2048]{1,0:T(8,128)} %refs_5_.1, f32[4096,2048]{1,0:T(8,128)} %refs_5_.1, f32[4096,2048]{1,0:T(8,128)} %refs_5_.1, f32[4096,2048]{1,0:T(8,128)} %refs_5_.1, ...), custom_call_target="tpu_custom_call" | custom-call | tf_op jit(solution)/shard_map/pallas_call | solution.py:288
  56.9 52.8 %shard_map.61 = (f32[2,48,512]{2,1,0:T(8,128)S(1)}, f32[2,16,512]{2,1,0:T(8,128)S(1)}) custom-call(f32[2,4,4,2,48,512]{5,4,3,2,1,0:T(8,128)S(1)} %bitcast.8, f32[2,4,4,2,16,512]{5,4,3,2,1,0:T(8,128)S(1)} %bitcast.9), custom_call_target="tpu_custom_call" | custom-call | tf_op jit(solution)/shard_map/pallas_call | solution.py:143
  109.7 0.0 copy-start
  109.7 0.6 copy-done
  110.3 0.0 copy-start.2
  110.3 0.0 copy-start.1
  110.3 20.0 %shard_map.62 = f32[2,4,4,2,16,512]{5,4,3,2,1,0:T(8,128)} custom-call(f32[2,16,512]{2,1,0:T(8,128)} %copy-done), custom_call_target="tpu_custom_call" | custom-call | tf_op jit(solution)/shard_map/pallas_call | solution.py:221
  130.3 0.0 copy-done.1
  130.3 0.6 bitcast_dynamic-update-slice_fusion
  131.0 0.0 copy-done.2
  131.0 3.4 %bitcast_subtract_fusion = f32[2,512,512]{2,1,0:T(8,128)} fusion(f32[2,512,512]{2,1,0:T(8,128)S(1)} %copy-done.2, f32[2,4,4,2,16,512]{5,4,3,2,1,0:T(8,128)} %bitcast_dynamic-update-slice_fusion), kind=kLoop, calls=%fused_computation | loop fusion | flops 524288 | bytes 6291456 | tf_op jit(solution)/shard_map/sub | solution.py:336
  134.4 0.7 copy.9
  (1 shorter events, 0.0 us)
Async XLA Ops:
  2.3 40.8 %copy-start.3 = (f32[2,384,512]{2,1,0:T(8,128)S(1)}, f32[2,384,512]{2,1,0:T(8,128)}, u32[]{:S(2)}) copy-start(f32[2,384,512]{2,1,0:T(8,128)} %param.5) | copy-start | bytes 4718596
  43.1 1.4 %copy-start.4 = (s32[2,6]{1,0:T(2,128)S(1)}, s32[2,6]{1,0:T(2,128)}, u32[]{:S(2)}) copy-start(s32[2,6]{1,0:T(2,128)} %param.7) | copy-start | bytes 148
  109.7 0.6 copy-start
  110.3 20.7 %copy-start.2 = (f32[2,512,512]{2,1,0:T(8,128)S(1)}, f32[2,512,512]{2,1,0:T(8,128)}, u32[]{:S(2)}) copy-start(f32[2,512,512]{2,1,0:T(8,128)} %param.6) | copy-start | bytes 6291460
  110.3 20.0 %copy-start.1 = (f32[2,16,512]{2,1,0:T(8,128)S(1)}, f32[2,16,512]{2,1,0:T(8,128)}, u32[]{:S(2)}) copy-start(f32[2,16,512]{2,1,0:T(8,128)} %copy-done) | copy-start | bytes 196612
